TPU v7x, 128 devices: a whole 4x4x4 slice. The times are simulated.
128 devices in a mesh: row: 8 (over y, z_lo), col: 8 (over x, core), feat: 2 (over z_hi).
Axes of the slice: x: 4, y: 4, z: 4 (z_hi: 2, z_lo: 2; z = z_hi * 2 + z_lo), core: 2. Of those that a mesh axis runs over, the one named last changes fastest.
Arguments:
- features: bfloat16 [32768, 128], P(('col', 'row')), may hold values from -6 to 6
- weight: bfloat16 [128, 256], P(None, 'feat'), may hold values from -0.5 to 0.5
- hidden_bias: float32 [256], P('feat'), may hold values from -4 to 4
- adjacency_tiles: bfloat16 [8, 8, 640, 128, 128], P('row', 'col'), may hold values from -0.078125 to 0.078125
- tile_rows: int32 [8, 8, 640], P('row', 'col'), may hold values from 0 to 31
- tile_columns: int32 [8, 8, 640], P('row', 'col'), may hold values from 0 to 31
- tile_count: int32 [8, 8], P('row', 'col'), may hold values from 1 to 640, as said below
- cotangent: bfloat16 [32768, 256], P(('row', 'col'), 'feat'), may hold values from -6 to 6
Outputs:
- activations: bfloat16 [32768, 256], P(('row', 'col'), 'feat')
- grad_features: float32 [32768, 128], P(('col', 'row'))
- grad_weight: float32 [128, 256], P(None, 'feat')
- grad_bias: float32 [256], P('feat')
Inputs may be any that keep to these rules, and one draw needn't show every extreme that they name: `tile_count`: tiles at or past this count on a device are ignored; some device uses all 640.
All inputs are finite; a program needn't handle non-finite values.
Results may differ from a plain program's by a relative error of at most 0.024.
Values may be sent and summed in bfloat16 or wider, within the bound.
No kernel may reach another device: no remote copies, remote signals or barrier semaphores. Data moves between devices by JAX's collectives and lax.ppermute only.
A program may use at most 128 MiB of HBM per device.

v0:
```python
import jax
import jax.numpy as jnp
from jax import lax
from jax.sharding import PartitionSpec as P


def silu_slope(values):
    sigma = jax.nn.sigmoid(values)
    return sigma * (1.0 + values * (1.0 - sigma))


def tile_products(tile_stack, take_index, put_index, count, source, out_blocks, flipped):
    group_size = 128
    tile_side = tile_stack.shape[-1]
    feature_width = source.shape[-1]

    def advance(index, running):
        first_tile = index * group_size
        tile_block = lax.dynamic_slice_in_dim(tile_stack, first_tile, group_size, 0)
        take_rows = lax.dynamic_slice_in_dim(take_index, first_tile, group_size, 0)
        put_rows = lax.dynamic_slice_in_dim(put_index, first_tile, group_size, 0)
        picked = jnp.take(source, take_rows, axis=0)
        if flipped:
            products = jnp.einsum(
                "tab,taw->tbw", tile_block, picked, preferred_element_type=jnp.float32
            )
        else:
            products = jnp.einsum(
                "tab,tbw->taw", tile_block, picked, preferred_element_type=jnp.float32
            )
        in_range = first_tile + jnp.arange(group_size, dtype=jnp.int32) < count
        products = jnp.where(in_range[:, None, None], products, jnp.float32(0.0))
        return running.at[put_rows].add(products)

    rounds = (count + group_size - 1) // group_size
    return lax.fori_loop(
        0, rounds, advance, jnp.zeros((out_blocks, tile_side, feature_width), jnp.float32)
    )


def local(
    features, weight, hidden_bias, adjacency_tiles, tile_rows, tile_columns, tile_count, cotangent
):
    tile_stack = adjacency_tiles[0, 0]
    row_blocks = tile_rows[0, 0]
    column_blocks = tile_columns[0, 0]
    count = tile_count[0, 0]
    tile_side = tile_stack.shape[-1]
    own_rows = features.shape[0]
    half_width = weight.shape[1]
    range_blocks = own_rows // tile_side * lax.axis_size("col")
    panel_blocks = own_rows // tile_side * lax.axis_size("row")
    projected = jnp.dot(features, weight, preferred_element_type=jnp.float32).astype(jnp.bfloat16)
    panel = lax.all_gather(projected, "row", axis=0, tiled=True).reshape(
        panel_blocks, tile_side, half_width
    )
    partial_sums = tile_products(
        tile_stack, column_blocks, row_blocks, count, panel, range_blocks, False
    )
    partial_sums = partial_sums.reshape(range_blocks * tile_side, half_width)
    preact = (
        lax.psum_scatter(
            partial_sums.astype(jnp.bfloat16), "col", scatter_dimension=0, tiled=True
        ).astype(jnp.float32)
        + hidden_bias
    )
    grad_pre = (cotangent.astype(jnp.float32) * silu_slope(preact)).astype(jnp.bfloat16)
    grad_range = lax.all_gather(grad_pre, "col", axis=0, tiled=True)
    activations = jax.nn.silu(preact).astype(jnp.bfloat16)
    grad_source = grad_range.reshape(range_blocks, tile_side, half_width)
    back_terms = tile_products(
        tile_stack, row_blocks, column_blocks, count, grad_source, panel_blocks, True
    )
    back_terms = back_terms.reshape(panel_blocks * tile_side, half_width)
    grad_projected = lax.psum_scatter(
        back_terms.astype(jnp.bfloat16), "row", scatter_dimension=0, tiled=True
    )
    local_weight = jnp.einsum(
        "nf,nh->fh", features, grad_projected, preferred_element_type=jnp.float32
    )
    local_bias = jnp.sum(grad_pre.astype(jnp.float32), axis=0)
    grad_weight, grad_bias = lax.psum((local_weight, local_bias), ("row", "col"))
    local_input = jnp.einsum(
        "nh,fh->nf", grad_projected, weight, preferred_element_type=jnp.float32
    )
    grad_features = lax.psum(local_input.astype(jnp.bfloat16), "feat").astype(jnp.float32)
    return (activations, grad_features, grad_weight, grad_bias)


def solution(mesh):
    placed = (
        P(("col", "row"), None),
        P(None, "feat"),
        P("feat"),
        P("row", "col", None, None, None),
        P("row", "col", None),
        P("row", "col", None),
        P("row", "col"),
        P(("row", "col"), "feat"),
    )
    return jax.shard_map(
        local,
        mesh=mesh,
        in_specs=placed,
        out_specs=(P(("row", "col"), "feat"), P(("col", "row"), None), P(None, "feat"), P("feat")),
        check_vma=False,
    )
```

profile of v0, /device:TPU:0, one launch (start us, length us, event | category | flops | bytes accessed | tf_op | source)
XLA Modules:
  0.0 967.7 jit_solution(8119670980813940387)
XLA Ops:
  7.2 0.0 copy-start
  7.2 0.0 all-gather.3.cloned.1.call-start
  7.2 0.8 copy-done
  8.1 1.6 convolution_convert_fusion.1
  9.7 0.0 all-gather.3.cloned.1.call-update
  9.7 0.0 reduce-scatter.3.cloned.1.call-start
  10.4 0.7 reduce
  11.1 0.7 reduce.1
  11.8 39.9 %all-gather.3.cloned.1.call-done = bf16[4096,128]{1,0:T(8,128)(2,1)} async-done(((bf16[512,128]{1,0:T(8,128)(2,1)}), bf16[4096,128]{1,0:T(8,128)(2,1)}) %all-gather.3.cloned.1.call-update) | async-done | bytes 1048592 | tf_op jit(solution)/shard_map/all_gather | solution.py:54
  51.7 0.2 broadcast.39.clone
  52.0 30.2 %while.20 = (s32[]{:T(128)}, f32[32,128,128]{2,1,0:T(8,128)S(1)}, s32[]{:T(128)}, s32[640]{0:T(1024)S(1)}, s32[]{:T(128)}, /*index=5*/bf16[640,128,128]{2,1,0:T(...) while((s32[]{:T(128)}, f32[32,128,128]{2,1,0:T(8,128)S(1)}, ...), condition=%wide.region_2.4_spmd, body=%wide.region_0.3_spmd.sunk | while | flops 543164800 | bytes 50340024 | solution.py:36
  52.0 0.7 compare_and_fusion.4
  52.7 4.3 gather_fusion
  57.0 8.0 broadcast_select_fusion.4
  65.0 0.1 compare_select_fusion.8
  65.1 17.1 %scatter_fusion = f32[32,128,128]{2,1,0:T(8,128)S(1)} fusion(f32[32,128,128]{2,1,0:T(8,128)S(1)} %get-tuple-element.271, s32[128]{0:T(128)S(1)} %compare_select_fusion.8, f32[128,128,128]{2,1,0:T(8,128)} %broadcast_select_fusion.4), kind=kCustom, calls=%fused_computation.2.clone.1 | custom fusion | flops 2097152 | bytes 25166336 | tf_op jit(solution)/shard_map/while/body/scatter-add | solution.py:33
  82.2 0.0 copy-start.2
  82.2 0.0 copy-start.3
  82.2 1.2 convert_element_type.37
  83.4 0.0 reduce-scatter.3.cloned.1.call-update
  83.4 0.0 all-gather.5.cloned.1.call-start
  83.4 151.7 %reduce-scatter.3.cloned.1.call-done = bf16[512,128]{1,0:T(8,128)(2,1)} async-done(((bf16[4096,128]{1,0:T(8,128)(2,1)}), bf16[512,128]{1,0:T(8,128)(2,1)}) %reduce-scatter.3.cloned.1.call-update) | async-done | bytes 131088 | tf_op jit(solution)/shard_map/reduce_scatter | solution.py:62
  235.1 0.0 copy-done.2
  235.1 0.0 copy-done.3
  235.1 1.7 convert_reduce_fusion
  236.8 0.0 all-gather.5.cloned.1.call-update
  236.9 0.0 reduce-scatter.5.cloned.1.call-start
  236.9 28.0 %copy.12 = bf16[1,1,640,128,128]{3,4,2,1,0:T(8,128)(2,1)} copy(bf16[1,1,640,128,128]{4,3,2,1,0:T(8,128)(2,1)} %bitcast.19) | data formatting | bytes 41943040 | tf_op args[3]
  264.9 0.0 all-gather.5.cloned.1.call-done
  264.9 0.2 broadcast.39
  265.2 30.2 %while.21 = (s32[]{:T(128)}, f32[32,128,128]{2,1,0:T(8,128)S(1)}, s32[]{:T(128)}, s32[640]{0:T(1024)S(1)}, s32[]{:T(128)}, /*index=5*/bf16[640,128,128]{1,2,0:T(...) while((s32[]{:T(128)}, f32[32,128,128]{2,1,0:T(8,128)S(1)}, ...), condition=%wide.region_6.8_spmd, body=%wide.region_4.7_spmd.sunk | while | flops 543164800 | bytes 50340024 | solution.py:36
  265.2 0.7 compare_and_fusion.5
  265.9 4.3 gather_fusion.1
  270.2 8.1 broadcast_select_fusion.5
  278.2 0.1 compare_select_fusion.9
  278.3 17.0 %scatter_fusion.1 = f32[32,128,128]{2,1,0:T(8,128)S(1)} fusion(f32[32,128,128]{2,1,0:T(8,128)S(1)} %get-tuple-element.307, s32[128]{0:T(128)S(1)} %compare_select_fusion.9, f32[128,128,128]{2,1,0:T(8,128)} %broadcast_select_fusion.5), kind=kCustom, calls=%fused_computation.3.clone.1 | custom fusion | flops 2097152 | bytes 25166336 | tf_op jit(solution)/shard_map/while/body/scatter-add | solution.py:33
  295.4 0.0 copy-start.1
  295.4 1.2 convert_element_type.43
  296.6 0.0 reduce-scatter.5.cloned.1.call-update
  296.6 0.0 all-reduce.5.cloned.1.call-start
  296.6 158.8 %reduce-scatter.5.cloned.1.call-done = bf16[512,128]{1,0:T(8,128)(2,1)} async-done(((bf16[4096,128]{1,0:T(8,128)(2,1)}), bf16[512,128]{1,0:T(8,128)(2,1)}) %reduce-scatter.5.cloned.1.call-update) | async-done | bytes 131088 | tf_op jit(solution)/shard_map/reduce_scatter | solution.py:75
  455.4 1.8 convolution_bitcast_fusion
  457.2 0.0 all-reduce.5.cloned.1.call-update
  457.2 0.0 all-reduce.3.cloned.1.call-start
  457.2 0.0 copy-done.1
  457.3 1.7 convolution_convert_fusion
  459.0 0.0 all-reduce.3.cloned.1.call-update
  459.0 138.9 %psum.23 = f32[128]{0:T(128)} all-reduce(f32[128]{0:T(128)S(1)} %get-tuple-element.141), channel_id=1, replica_groups=mesh['row'=8,'col'=8,'feat'=2] {'row','col'}, use_global_device_ids=true, to_apply=%region_11.13 | all-reduce | flops 128 | bytes 1024 | tf_op jit(solution)/shard_map/psum | solution.py:82
  598.0 332.2 %all-reduce.5.cloned.1.call-done = f32[128,128]{0,1:T(8,128)} async-done(((f32[128,128]{0,1:T(8,128)}), f32[128,128]{0,1:T(8,128)}) %all-reduce.5.cloned.1.call-update) | async-done | bytes 65552 | tf_op jit(solution)/shard_map/psum | solution.py:82
  930.2 1.6 copy.14
  931.8 27.5 %all-reduce.3.cloned.1.call-done = bf16[512,128]{1,0:T(8,128)(2,1)} async-done(((bf16[512,128]{1,0:T(8,128)(2,1)}), bf16[512,128]{1,0:T(8,128)(2,1)}) %all-reduce.3.cloned.1.call-update) | async-done | bytes 131088 | tf_op jit(solution)/shard_map/psum | solution.py:86
  959.3 1.6 convert_element_type.46
  (2 shorter events, 0.0 us)
Async XLA Ops:
  7.2 0.9 copy-start
  7.2 44.6 %all-gather.3.cloned.1.call-start = ((), (), s32[]{:S(2)}) async-start(), calls=%async_computation.2 | async-start | bytes 1179648 | tf_op jit(solution)/shard_map/all_gather | solution.py:54
  9.7 225.4 %reduce-scatter.3.cloned.1.call-start = ((), (), s32[]{:S(2)}) async-start(), calls=%async_computation.3 | async-start | bytes 1179648 | tf_op jit(solution)/shard_map/reduce_scatter | solution.py:62
  82.2 152.9 %copy-start.2 = (bf16[512,128]{1,0:T(8,128)(2,1)S(1)}, bf16[512,128]{1,0:T(8,128)(2,1)}, u32[]{:S(2)}) copy-start(bf16[512,128]{1,0:T(8,128)(2,1)} %param.21) | copy-start | bytes 393220
  82.2 152.9 %copy-start.3 = (f32[128]{0:T(128)S(1)}, f32[128]{0:T(128)}, u32[]{:S(2)}) copy-start(f32[128]{0:T(128)} %param.16) | copy-start | bytes 1540
  83.4 181.5 %all-gather.5.cloned.1.call-start = ((), (), s32[]{:S(2)}) async-start(), calls=%async_computation.4 | async-start | bytes 1179648 | tf_op jit(solution)/shard_map/all_gather | solution.py:68
  236.9 218.5 %reduce-scatter.5.cloned.1.call-start = ((), (), s32[]{:S(2)}) async-start(), calls=%async_computation.5 | async-start | bytes 1179648 | tf_op jit(solution)/shard_map/reduce_scatter | solution.py:75
  295.4 161.9 %copy-start.1 = (bf16[128,128]{1,0:T(8,128)(2,1)S(1)}, bf16[128,128]{1,0:T(8,128)(2,1)}, u32[]{:S(2)}) copy-start(bf16[128,128]{1,0:T(8,128)(2,1)} %param.15) | copy-start | bytes 98308
  296.6 633.6 %all-reduce.5.cloned.1.call-start = ((), (), s32[]{:S(2)}) async-start(), calls=%async_computation.7 | async-start | bytes 131072 | tf_op jit(solution)/shard_map/psum | solution.py:82
  457.2 502.1 %all-reduce.3.cloned.1.call-start = ((), (), s32[]{:S(2)}) async-start(), calls=%async_computation.6 | async-start | bytes 262144 | tf_op jit(solution)/shard_map/psum | solution.py:86
Sparse Core Ops, SparseCore 0:
  10.2 41.4 all-gather.2
  83.5 151.5 reduce-scatter.2
  237.4 22.1 all-gather.4
  296.7 158.6 reduce-scatter.4
  458.3 471.8 all-reduce.4
  933.2 26.0 all-reduce.2
where the time goes:
time: 973 us; the launch traced here: 968 us
  waiting for transfers between devices  710 us (73%)
  blocking collectives  139 us (14%)
  other arithmetic  42.8 us (4%)
  local copies, waits for them, and re-layouts  39.4 us (4%)
  matrix products  21.2 us (2%)
  between operations  14.9 us (2%)
    psum x1, waiting for transfers between devices, local(): lax.psum((local_weight, local_bias), ('row', 'col'))  332 us
    reduce_scatter x1, waiting for transfers between devices, local(): lax.psum_scatter(back_terms.astype(jnp.bfloat16), 'row', scatter_dimensio...  159 us
    reduce_scatter x1, waiting for transfers between devices, local(): lax.psum_scatter(partial_sums.astype(jnp.bfloat16), 'col', scatter_dimens...  152 us
    psum x1, blocking collectives, local(): lax.psum((local_weight, local_bias), ('row', 'col'))  139 us
    all_gather x1, waiting for transfers between devices, local(): lax.all_gather(projected, 'row', axis=0, tiled=True)  39.9 us
    scatter-add x2, other arithmetic, advance(): return running.at[put_rows].add(products)  34.1 us
    unnamed x10, local copies, waits for them, and re-layouts  30.4 us
    psum x1, waiting for transfers between devices, local(): lax.psum(local_input.astype(jnp.bfloat16), 'feat').astype(jnp.float32)  27.5 us
  transfers between devices with their start and end apart: 6, of which 5 were waited for; matrix products, arithmetic and copies ran while one was open for 3% of the time, Pallas kernels for 0%

commit v1 on v0

v1 whole, which is shorter than its diff:
```python
import functools

import jax
import jax.numpy as jnp
from jax import lax
from jax.experimental import pallas as pl
from jax.experimental.pallas import tpu as pltpu
from jax.sharding import PartitionSpec as P

F32 = jnp.float32
BF16 = jnp.bfloat16
TILE = 128
GROUP = 8
AHEAD = 8
SLOTS = AHEAD + 1
VMEM = pl.BlockSpec(memory_space=pltpu.VMEM)
SMEM = pl.BlockSpec(memory_space=pltpu.SMEM)
ANY = pl.BlockSpec(memory_space=pl.ANY)
PARAMS = pltpu.CompilerParams(vmem_limit_bytes=24 * 1024 * 1024)


def swap(values, axis, mask):
    size = lax.axis_size(axis)
    return lax.ppermute(values, axis, [(i, i ^ mask) for i in range(size)])


def exchange(parts, axis):
    return lax.all_to_all(parts, axis, 0, 0)


def pick_kernel(n_out, n_back, meta, rows, columns, forward, backward, groups):
    half = meta[1]

    def step(t, n):
        column = columns[t]
        row = rows[t]
        place = (column >> 2) * 2 + (column & 1)
        forward[n] = t + place * 1024 + row * 65536
        backward[n] = t + row * 1024 + place * 65536
        return n + ((column >> 1) & 1 == half).astype(jnp.int32)

    n = lax.fori_loop(0, meta[0], step, jnp.int32(0))
    for j in range(GROUP):
        forward[n + j] = n_out * 65536
        backward[n + j] = n_back * 65536
    groups[0] = (n + GROUP - 1) // GROUP


def pick(meta, rows, columns, n_out, n_back):
    length = rows.shape[0] + GROUP
    return pl.pallas_call(
        functools.partial(pick_kernel, n_out, n_back),
        out_shape=[
            jax.ShapeDtypeStruct((length,), jnp.int32),
            jax.ShapeDtypeStruct((length,), jnp.int32),
            jax.ShapeDtypeStruct((1,), jnp.int32),
        ],
        in_specs=[SMEM] * 3,
        out_specs=[SMEM] * 3,
        name="pick_tiles",
    )(meta, rows, columns)


def tiles_kernel(flipped, n_out, groups, picked, tiles, source, out, held, total, arrived):
    count = groups[0]

    def fetch(g):
        slot = lax.rem(g, SLOTS)
        for j in range(GROUP):
            t = picked[g * GROUP + j] & 1023
            pltpu.make_async_copy(tiles.at[t], held.at[slot * GROUP + j], arrived.at[slot]).start()

    def first(g, carry):
        fetch(g)
        return carry

    lax.fori_loop(0, jnp.minimum(count, AHEAD), first, 0)
    total[...] = jnp.zeros_like(total)

    def step(g, carry):
        @pl.when(g + AHEAD < count)
        def _():
            fetch(g + AHEAD)

        slot = lax.rem(g, SLOTS)
        block = held.at[pl.ds(slot * GROUP, GROUP)]
        pltpu.make_async_copy(tiles.at[pl.ds(0, GROUP)], block, arrived.at[slot]).wait()
        places = []
        products = []
        for j in range(GROUP):
            code = picked[g * GROUP + j]
            places.append(code >> 16)
            tile = held[slot * GROUP + j]
            other = source[(code >> 10) & 63]
            pair = (other, tile) if flipped else (tile, other)
            products.append(jnp.dot(*pair, preferred_element_type=F32))
        for place, product in zip(places, products):
            total[place] += product
        return carry

    lax.fori_loop(0, count, step, 0)
    out[...] = total[:n_out].astype(BF16)


def tile_sums(groups, picked, tiles, source, n_out, flipped):
    return pl.pallas_call(
        functools.partial(tiles_kernel, flipped, n_out),
        out_shape=jax.ShapeDtypeStruct((n_out, TILE, TILE), BF16),
        in_specs=[SMEM, SMEM, ANY, VMEM],
        out_specs=VMEM,
        scratch_shapes=[
            pltpu.VMEM((SLOTS * GROUP, TILE, TILE), BF16),
            pltpu.VMEM((n_out + 1, TILE, TILE), F32),
            pltpu.SemaphoreType.DMA((SLOTS,)),
        ],
        compiler_params=PARAMS,
        cost_estimate=pl.CostEstimate(
            flops=320 * 2 * TILE**3, bytes_accessed=320 * 2 * TILE**2, transcendentals=0
        ),
        name="tiles_backward" if flipped else "tiles_forward",
    )(groups, picked, tiles, source)


def gather_sum_kernel(parts, total, sent):
    value = jnp.sum(parts[...].astype(F32), axis=0)
    total[...] = value
    sent[...] = value.astype(BF16)


def gather_sum(parts):
    shape = parts.shape[1:]
    return pl.pallas_call(
        gather_sum_kernel,
        out_shape=[jax.ShapeDtypeStruct(shape, F32), jax.ShapeDtypeStruct(shape, BF16)],
        in_specs=[VMEM],
        out_specs=[VMEM] * 2,
        compiler_params=PARAMS,
        name="sum_parts",
    )(parts)


def middle_kernel(own, other, weight, bias, cotangent, activations, back_source, grad_weight, grad_bias):
    sums = (own[...] + other[...].astype(F32)).astype(BF16)
    preact = jnp.dot(sums, weight[...], preferred_element_type=F32) + bias[...]
    sigma = jax.nn.sigmoid(preact)
    activations[...] = (preact * sigma).astype(BF16)
    grad = cotangent[...].astype(F32) * (sigma * (1.0 + preact * (1.0 - sigma)))
    grad_pre = grad.astype(BF16)
    grad_bias[...] = jnp.sum(grad_pre.astype(F32), axis=0, keepdims=True)
    grad_weight[...] = lax.dot_general(
        sums, grad_pre, (((0,), (0,)), ((), ())), preferred_element_type=F32
    )
    for b in range(back_source.shape[0]):
        back_source[b] = lax.dot_general(
            weight[...],
            grad_pre[b * TILE : (b + 1) * TILE],
            (((1,), (1,)), ((), ())),
            preferred_element_type=F32,
        )


def middle(own, other, weight, bias, cotangent):
    rows, width = cotangent.shape
    return pl.pallas_call(
        middle_kernel,
        out_shape=[
            jax.ShapeDtypeStruct((rows, width), BF16),
            jax.ShapeDtypeStruct((rows // TILE, weight.shape[0], TILE), F32),
            jax.ShapeDtypeStruct(weight.shape, F32),
            jax.ShapeDtypeStruct((1, width), F32),
        ],
        in_specs=[VMEM] * 5,
        out_specs=[VMEM] * 4,
        compiler_params=PARAMS,
        name="middle",
    )(own, other, weight, bias, cotangent)


def final_kernel(parts, total, sent):
    for b in range(parts.shape[1]):
        value = jnp.sum(parts[:, b].astype(F32), axis=0).T
        total[b] = value
        sent[b] = value.astype(BF16)


def final_sum(parts):
    shape = parts.shape[1:]
    return pl.pallas_call(
        final_kernel,
        out_shape=[jax.ShapeDtypeStruct(shape, F32), jax.ShapeDtypeStruct(shape, BF16)],
        in_specs=[VMEM],
        out_specs=[VMEM] * 2,
        compiler_params=PARAMS,
        name="final_sum",
    )(parts)


def local(
    features, weight, hidden_bias, adjacency_tiles, tile_rows, tile_columns, tile_count, cotangent
):
    tiles = adjacency_tiles[0, 0]
    n_row, n_col = lax.axis_size("row"), lax.axis_size("col")
    half = lax.axis_index("feat")
    own_rows, fin = features.shape
    blocks = own_rows // TILE
    n_out, n_back = blocks * n_col, blocks // 2 * n_row
    meta = jnp.stack([tile_count[0, 0], half.astype(jnp.int32)])
    forward, backward, groups = pick(meta, tile_rows[0, 0], tile_columns[0, 0], n_out, n_back)

    mine = lax.dynamic_slice_in_dim(features, half * (own_rows // 2), own_rows // 2, 0)
    panel = exchange(jnp.broadcast_to(mine[None], (n_row,) + mine.shape), "row")
    panel = panel.reshape(n_back, TILE, fin)
    partial_sums = tile_sums(groups, forward, tiles, panel, n_out, False)
    parts = exchange(partial_sums.reshape(n_col, own_rows, fin), "col")
    own, sent = gather_sum(parts)
    other = swap(sent, "feat", 1)
    activations, back_own, local_weight, local_bias = middle(
        own, other, weight, hidden_bias[None], cotangent
    )
    back_source = (back_own + swap(back_own.astype(BF16), "feat", 1).astype(F32)).astype(BF16)
    back_range = lax.all_gather(back_source, "col", axis=0, tiled=False)
    back_range = back_range.reshape(n_out, fin, TILE)

    grads = jnp.concatenate([local_weight, jnp.broadcast_to(local_bias, (8, local_bias.shape[1]))], 0)
    for axis in ("col", "row"):
        for mask in (1, 2, 4):
            grads = grads + swap(grads, axis, mask)

    back = tile_sums(groups, backward, tiles, back_range, n_back, True)
    back_parts = exchange(back.reshape(n_row, blocks // 2, fin, TILE), "row")
    own_grad, sent_grad = final_sum(back_parts)
    other_grad = swap(sent_grad, "feat", 1).astype(F32)
    own_grad = own_grad.reshape(own_rows // 2, fin)
    other_grad = other_grad.reshape(own_rows // 2, fin)
    grad_features = jnp.where(
        half == 0,
        jnp.concatenate([own_grad, other_grad], 0),
        jnp.concatenate([other_grad, own_grad], 0),
    )
    return (activations, grad_features, grads[:fin], grads[fin])


def solution(mesh):
    placed = (
        P(("col", "row"), None),
        P(None, "feat"),
        P("feat"),
        P("row", "col", None, None, None),
        P("row", "col", None),
        P("row", "col", None),
        P("row", "col"),
        P(("row", "col"), "feat"),
    )
    return jax.shard_map(
        local,
        mesh=mesh,
        in_specs=placed,
        out_specs=(P(("row", "col"), "feat"), P(("col", "row"), None), P(None, "feat"), P("feat")),
        check_vma=False,
    )
```

time: 973 us -> 203 us (0.21)
  waiting for transfers between devices: 710 us -> 54.4 us
  blocking collectives: 139 us -> 45.1 us
  starting transfers between devices: 0.25 us -> 48.9 us
  other arithmetic: 42.8 us -> 4.7 us
  matrix products: 21.2 us -> 0 us
  local copies, waits for them, and re-layouts: 39.4 us -> 18.7 us
  Pallas kernels: 0 us -> 16.7 us
    psum x2 -> x0, waiting for transfers between devices: 360 us -> none  [the longest x1 332 us: local(): lax.psum((local_weight, local_bias), ('row', 'col'))]
    reduce_scatter x2 -> x0, waiting for transfers between devices: 310 us -> none  [the longest x1 159 us: local(): lax.psum_scatter(back_terms.astype(jnp.bfloat16), 'row', scatter_dimensio...]
    psum x1 -> x0, blocking collectives: 139 us -> none  [local(): lax.psum((local_weight, local_bias), ('row', 'col'))]
    all_to_all x0 -> x1, blocking collectives: none -> 45.1 us  [exchange(): return lax.all_to_all(parts, axis, 0, 0)]
    scatter-add x2 -> x0, other arithmetic: 34.1 us -> none  [advance(): return running.at[put_rows].add(products)]
    all_to_all x0 -> x2, starting transfers between devices: none -> 33.2 us  [exchange(): return lax.all_to_all(parts, axis, 0, 0)]
    ppermute x0 -> x9, waiting for transfers between devices: none -> 27.5 us  [swap(): return lax.ppermute(values, axis, [(i, i ^ mask) for i in range(size)])]
    dot_general x5 -> x0, matrix products: 21.2 us -> none  [the longest x1 8.07 us: advance(): jnp.einsum('tab,taw->tbw', tile_block, picked, preferred_element_type=jnp...]
  transfers between devices with their start and end apart: 6 -> 12, of which waited for: 5 -> 10; matrix products, arithmetic and copies ran while one was open for 3% -> 2% of each run, Pallas kernels for 0% -> 5%
where the time goes in v1:
time: 203 us
  waiting for transfers between devices  54.4 us (27%)
  starting transfers between devices  48.9 us (24%)
  blocking collectives  45.1 us (22%)
  local copies, waits for them, and re-layouts  18.7 us (9%)
  Pallas kernels  16.7 us (8%)
  between operations  14.8 us (7%)
  other arithmetic  4.7 us (2%)
    all_to_all x1, blocking collectives, exchange(): return lax.all_to_all(parts, axis, 0, 0)  45.1 us
    all_to_all x2, starting transfers between devices, exchange(): return lax.all_to_all(parts, axis, 0, 0)  33.2 us
    ppermute x9, waiting for transfers between devices, swap(): return lax.ppermute(values, axis, [(i, i ^ mask) for i in range(size)])  27.5 us
    all_gather x1, waiting for transfers between devices, local(): back_range = lax.all_gather(back_source, 'col', axis=0, tiled=False)  24.2 us
    unnamed x18, local copies, waits for them, and re-layouts  16.7 us
    ppermute x9, starting transfers between devices, swap(): return lax.ppermute(values, axis, [(i, i ^ mask) for i in range(size)])  15.7 us
    pallas_call x2, Pallas kernels, tile_sums(): pl.pallas_call(functools.partial(tiles_kernel, flipped, n_out), out_shape...  12.6 us
  transfers between devices with their start and end apart: 12, of which 10 were waited for; matrix products, arithmetic and copies ran while one was open for 2% of the time, Pallas kernels for 5%

profile of v1, /device:TPU:0, one launch (start us, length us, event | category | flops | bytes accessed | tf_op | source)
XLA Modules:
  0.0 203.5 jit_solution(15172295474607298249)
XLA Ops:
  7.2 0.0 copy-start
  7.2 0.0 copy-start.4
  7.2 0.0 copy-start.8
  7.2 0.0 copy-start.5
  7.2 0.9 copy-done
  8.1 0.9 broadcast_in_dim.16
  9.0 5.9 %all-to-all-start = ((bf16[8,256,128]{2,1,0:T(8,128)(2,1)}), bf16[8,256,128]{2,1,0:T(8,128)(2,1)S(1)}, u32[]{:S(2)}, u32[]{:S(2)}) async-start(bf16[8,256,128]{2,1,0:T(8,128)(2,1)} %broadcast_in_dim.16), calls=%async_computation | async-start | bytes 1048576 | tf_op jit(solution)/shard_map/all_to_all | solution.py:28
  14.9 0.0 all-gather.3.cloned.1.call-start
  15.6 1.3 reduce.rows
  16.8 1.3 reduce.1.columns
  18.1 0.6 pad_add_fusion.meta
  18.7 2.9 %pick_tiles.1 = (s32[648]{0:T(1024)}, s32[648]{0:T(1024)}, s32[1]{0:T(128)}) custom-call(s32[2]{0:T(128)} %pad_add_fusion.meta, s32[640]{0:T(1024)} %reduce.rows, s32[640]{0:T(1024)} %reduce.1.columns), custom_call_target="tpu_custom_call" | custom-call | tf_op jit(solution)/shard_map/pick_tiles/pallas_call | solution.py:51
  21.6 0.0 copy-start.6
  21.6 2.7 %all-to-all-done = bf16[8,256,128]{2,1,0:T(8,128)(2,1)S(1)} async-done(((bf16[8,256,128]{2,1,0:T(8,128)(2,1)}), bf16[8,256,128]{2,1,0:T(8,128)(2,1)S(1)}, u32[]{:S(2)}, u32[]{:S(2)}) %all-to-all-start) | async-done | bytes 524320 | tf_op jit(solution)/shard_map/all_to_all | solution.py:28
  24.3 0.0 copy-start.1
  24.3 7.0 %copy-done.1 = bf16[1,1,640,128,128]{4,3,2,1,0:T(8,128)(2,1)S(1)} copy-done((bf16[1,1,640,128,128]{4,3,2,1,0:T(8,128)(2,1)S(1)}, bf16[1,1,640,128,128]{4,3,2,1,0:T(8,128)(2,1)}, u32[]{:S(2)}) %copy-start.1) | copy-done | bytes 20971544
  31.3 0.0 copy-start.7
  31.3 0.7 copy-done.7
  32.0 5.9 %tiles_forward.1 = bf16[32,128,128]{2,1,0:T(8,128)(2,1)S(1)} custom-call(s32[1]{0:T(128)} %get-tuple-element.15.groups, s32[648]{0:T(1024)S(1)} %copy-done.7, bf16[640,128,128]{2,1,0:T(8,128)(2,1)S(1)} %bitcast.15, bf16[16,128,128]{2,1,0:T(8,128)(2,1)S(1)} %bitcast.18), custom_call_target="tpu_custom_call" | custom-call | flops 1342177280 | bytes 10485760 | tf_op jit(solution)/shard_map/tiles_forward/pallas_call | solution.py:106
  37.9 45.1 %all_to_all.15.parts = bf16[8,512,128]{2,1,0:T(8,128)(2,1)S(1)} all-to-all(bf16[8,512,128]{2,1,0:T(8,128)(2,1)S(1)} %bitcast.17), channel_id=1, replica_groups=mesh['row'=8,'col'=8,'feat'=2] {'col'}, dimensions={0} | all-to-all | bytes 2097152 | tf_op jit(solution)/shard_map/all_to_all | solution.py:28
  83.1 0.1 sum_parts.1
  83.2 3.3 %collective-permute-start = (bf16[512,128]{1,0:T(8,128)(2,1)S(1)}, bf16[512,128]{1,0:T(8,128)(2,1)S(1)}, u32[]{:S(2)}, u32[]{:S(2)}) collective-permute-start(bf16[512,128]{1,0:T(8,128)(2,1)S(1)} %get-tuple-element.18), channel_id=1, source_target_pairs={{0,1},{1,0},{2,3},{3,2},{4,5},{5,4},{6,7},{7,6},{8,9},{9,8},{10,11... | collective-permute-start | bytes 393224 | tf_op jit(solution)/shard_map/ppermute | solution.py:24
  86.4 3.3 %collective-permute-done.other = bf16[512,128]{1,0:T(8,128)(2,1)S(1)} collective-permute-done((bf16[512,128]{1,0:T(8,128)(2,1)S(1)}, bf16[512,128]{1,0:T(8,128)(2,1)S(1)}, u32[]{:S(2)}, u32[]{:S(2)}) %collective-permute-start) | collective-permute-done | bytes 131104 | tf_op jit(solution)/shard_map/ppermute | solution.py:24
  89.7 0.0 copy-done.4
  89.7 0.0 copy-done.8
  89.8 0.0 copy-done.5
  89.8 0.9 middle.1
  90.7 3.3 %collective-permute-start.1 = (bf16[4,128,128]{2,1,0:T(8,128)(2,1)S(1)}, bf16[4,128,128]{2,1,0:T(8,128)(2,1)S(1)}, u32[]{:S(2)}, u32[]{:S(2)}) collective-permute-start(bf16[4,128,128]{2,1,0:T(8,128)(2,1)S(1)} %convert_element_type.10), channel_id=1, source_target_pairs={{0,1},{1,0},{2,3},{3,2},{4,5},{5,4},{6,7},{7,6},{8,9},{9,8},{10,11... | collective-permute-start | bytes 393224 | tf_op jit(solution)/shard_map/ppermute | solution.py:24
  93.9 3.3 %collective-permute-done.1 = bf16[4,128,128]{2,1,0:T(8,128)(2,1)S(1)} collective-permute-done((bf16[4,128,128]{2,1,0:T(8,128)(2,1)S(1)}, bf16[4,128,128]{2,1,0:T(8,128)(2,1)S(1)}, u32[]{:S(2)}, u32[]{:S(2)}) %collective-permute-start.1) | collective-permute-done | bytes 131104 | tf_op jit(solution)/shard_map/ppermute | solution.py:24
  97.2 0.7 add_convert_fusion
  97.9 0.0 all-gather.3.cloned.1.call-update
  98.0 0.1 collective-permute-start.3
  98.1 24.2 %all-gather.3.cloned.1.call-done.source = bf16[32,128,128]{2,1,0:T(8,128)(2,1)} async-done(((bf16[4,128,128]{2,1,0:T(8,128)(2,1)}), bf16[32,128,128]{2,1,0:T(8,128)(2,1)}) %all-gather.3.cloned.1.call-update) | async-done | bytes 1048592 | tf_op jit(solution)/shard_map/all_gather | solution.py:221
  122.2 0.0 copy-done.6
  122.2 0.0 copy-start.2
  122.2 7.0 %copy-done.2 = bf16[1,1,640,128,128]{4,3,2,1,0:T(8,128)(2,1)S(1)} copy-done((bf16[1,1,640,128,128]{4,3,2,1,0:T(8,128)(2,1)S(1)}, bf16[1,1,640,128,128]{4,3,2,1,0:T(8,128)(2,1)}, u32[]{:S(2)}) %copy-start.2) | copy-done | bytes 20971544
  129.2 0.0 copy-start.3
  129.2 1.2 copy-done.3
  130.4 6.7 %tiles_backward.1 = bf16[16,128,128]{2,1,0:T(8,128)(2,1)} custom-call(s32[1]{0:T(128)} %get-tuple-element.15.groups, s32[648]{0:T(1024)S(1)} %copy-done.6, bf16[640,128,128]{2,1,0:T(8,128)(2,1)S(1)} %bitcast.16, bf16[32,128,128]{2,1,0:T(8,128)(2,1)S(1)} %copy-done.3), custom_call_target="tpu_custom_call" | custom-call | flops 1342177280 | bytes 10485760 | tf_op jit(solution)/shard_map/tiles_backward/pallas_call | solution.py:106
  137.1 27.3 %all-to-all-start.2 = ((bf16[8,2,128,128]{3,2,1,0:T(8,128)(2,1)}), bf16[8,2,128,128]{3,2,1,0:T(8,128)(2,1)S(1)}, u32[]{:S(2)}, u32[]{:S(2)}) async-start(bf16[8,2,128,128]{3,2,1,0:T(8,128)(2,1)} %bitcast.6), calls=%async_computation.2 | async-start | bytes 1048576 | tf_op jit(solution)/shard_map/all_to_all | solution.py:28
  164.4 0.0 collective-permute-done.3
  164.4 0.1 collective-permute-start.4
  164.5 4.3 %collective-permute-done.4 = f32[136,128]{1,0:T(8,128)S(1)} collective-permute-done((f32[136,128]{1,0:T(8,128)S(1)}, f32[136,128]{1,0:T(8,128)S(1)}, u32[]{:S(2)}, u32[]{:S(2)}) %collective-permute-start.4) | collective-permute-done | bytes 69664 | tf_op jit(solution)/shard_map/ppermute | solution.py:24
  168.8 0.1 collective-permute-start.5
  168.9 5.8 %collective-permute-done.5 = f32[136,128]{1,0:T(8,128)S(1)} collective-permute-done((f32[136,128]{1,0:T(8,128)S(1)}, f32[136,128]{1,0:T(8,128)S(1)}, u32[]{:S(2)}, u32[]{:S(2)}) %collective-permute-start.5) | collective-permute-done | bytes 69664 | tf_op jit(solution)/shard_map/ppermute | solution.py:24
  174.7 2.5 %collective-permute-start.6 = (f32[136,128]{1,0:T(8,128)S(1)}, f32[136,128]{1,0:T(8,128)S(1)}, u32[]{:S(2)}, u32[]{:S(2)}) collective-permute-start(f32[136,128]{1,0:T(8,128)S(1)} %add.28), channel_id=1, source_target_pairs={{0,16},{16,0},{32,48},{48,32},{64,80},{80,64},{96,112},{112,96},{1... | collective-permute-start | bytes 208904 | tf_op jit(solution)/shard_map/ppermute | solution.py:24
  177.2 2.3 %collective-permute-done.6 = f32[136,128]{1,0:T(8,128)S(1)} collective-permute-done((f32[136,128]{1,0:T(8,128)S(1)}, f32[136,128]{1,0:T(8,128)S(1)}, u32[]{:S(2)}, u32[]{:S(2)}) %collective-permute-start.6) | collective-permute-done | bytes 69664 | tf_op jit(solution)/shard_map/ppermute | solution.py:24
  179.5 2.1 %collective-permute-start.7 = (f32[136,128]{1,0:T(8,128)S(1)}, f32[136,128]{1,0:T(8,128)S(1)}, u32[]{:S(2)}, u32[]{:S(2)}) collective-permute-start(f32[136,128]{1,0:T(8,128)S(1)} %add.29), channel_id=1, source_target_pairs={{0,32},{16,48},{32,0},{48,16},{64,96},{80,112},{96,64},{112,80},{1... | collective-permute-start | bytes 208904 | tf_op jit(solution)/shard_map/ppermute | solution.py:24
  181.6 2.3 %collective-permute-done.7 = f32[136,128]{1,0:T(8,128)S(1)} collective-permute-done((f32[136,128]{1,0:T(8,128)S(1)}, f32[136,128]{1,0:T(8,128)S(1)}, u32[]{:S(2)}, u32[]{:S(2)}) %collective-permute-start.7) | collective-permute-done | bytes 69664 | tf_op jit(solution)/shard_map/ppermute | solution.py:24
  183.9 3.6 %collective-permute-start.8 = (f32[136,128]{1,0:T(8,128)S(1)}, f32[136,128]{1,0:T(8,128)S(1)}, u32[]{:S(2)}, u32[]{:S(2)}) collective-permute-start(f32[136,128]{1,0:T(8,128)S(1)} %add.30), channel_id=1, source_target_pairs={{0,64},{16,80},{32,96},{48,112},{64,0},{80,16},{96,32},{112,48},{1... | collective-permute-start | bytes 208904 | tf_op jit(solution)/shard_map/ppermute | solution.py:24
  187.6 2.3 %collective-permute-done.8 = f32[136,128]{1,0:T(8,128)S(1)} collective-permute-done((f32[136,128]{1,0:T(8,128)S(1)}, f32[136,128]{1,0:T(8,128)S(1)}, u32[]{:S(2)}, u32[]{:S(2)}) %collective-permute-start.8) | collective-permute-done | bytes 69664 | tf_op jit(solution)/shard_map/ppermute | solution.py:24
  189.9 0.0 all-to-all-done.2.parts
  189.9 0.1 final_sum.1
  190.0 0.7 collective-permute-start.2
  190.7 0.5 slice_bitcast_fusion
  191.3 0.6 slice.8
  191.9 4.0 %collective-permute-done.2 = bf16[2,128,128]{2,1,0:T(8,128)(2,1)S(1)} collective-permute-done((bf16[2,128,128]{2,1,0:T(8,128)(2,1)S(1)}, bf16[2,128,128]{2,1,0:T(8,128)(2,1)S(1)}, u32[]{:S(2)}, u32[]{:S(2)}) %collective-permute-start.2) | collective-permute-done | bytes 65568 | tf_op jit(solution)/shard_map/ppermute | solution.py:24
  195.9 0.7 maximum_select_fusion
  (11 shorter events, 0.1 us)
Async XLA Ops:
  7.2 0.9 copy-start
  7.2 82.6 %copy-start.4 = (bf16[512,128]{1,0:T(8,128)(2,1)S(1)}, bf16[512,128]{1,0:T(8,128)(2,1)}, u32[]{:S(2)}) copy-start(bf16[512,128]{1,0:T(8,128)(2,1)} %cotangent.1) | copy-start | bytes 393220
  7.2 82.6 %copy-start.8 = (f32[128]{0:T(128)S(1)}, f32[128]{0:T(128)}, u32[]{:S(2)}) copy-start(f32[128]{0:T(128)} %param.10) | copy-start | bytes 1540
  7.2 82.6 %copy-start.5 = (bf16[128,128]{1,0:T(8,128)(2,1)S(1)}, bf16[128,128]{1,0:T(8,128)(2,1)}, u32[]{:S(2)}) copy-start(bf16[128,128]{1,0:T(8,128)(2,1)} %weight.1) | copy-start | bytes 98308
  9.0 15.4 %all-to-all-start = ((bf16[8,256,128]{2,1,0:T(8,128)(2,1)}), bf16[8,256,128]{2,1,0:T(8,128)(2,1)S(1)}, u32[]{:S(2)}, u32[]{:S(2)}) async-start(bf16[8,256,128]{2,1,0:T(8,128)(2,1)} %broadcast_in_dim.16), calls=%async_computation | async-start | bytes 1048576 | tf_op jit(solution)/shard_map/all_to_all | solution.py:28
  14.9 107.4 %all-gather.3.cloned.1.call-start = ((), (), s32[]{:S(2)}) async-start(), calls=%async_computation.3 | async-start | bytes 1179648 | tf_op jit(solution)/shard_map/all_gather | solution.py:221
  21.6 100.6 %copy-start.6 = (s32[648]{0:T(1024)S(1)}, s32[648]{0:T(1024)}, u32[]{:S(2)}) copy-start(s32[648]{0:T(1024)} %get-tuple-element.20.picked) | copy-start | bytes 7780
  24.3 7.0 %copy-start.1 = (bf16[1,1,640,128,128]{4,3,2,1,0:T(8,128)(2,1)S(1)}, bf16[1,1,640,128,128]{4,3,2,1,0:T(8,128)(2,1)}, u32[]{:S(2)}) copy-start(bf16[1,1,640,128,128]{4,3,2,1,0:T(8,128)(2,1)} %param.11) | copy-start | bytes 62914564
  31.3 0.7 copy-start.7
  83.2 6.6 %collective-permute-start = (bf16[512,128]{1,0:T(8,128)(2,1)S(1)}, bf16[512,128]{1,0:T(8,128)(2,1)S(1)}, u32[]{:S(2)}, u32[]{:S(2)}) collective-permute-start(bf16[512,128]{1,0:T(8,128)(2,1)S(1)} %get-tuple-element.18), channel_id=1, source_target_pairs={{0,1},{1,0},{2,3},{3,2},{4,5},{5,4},{6,7},{7,6},{8,9},{9,8},{10,11... | collective-permute-start | bytes 393224 | tf_op jit(solution)/shard_map/ppermute | solution.py:24
  90.7 6.6 %collective-permute-start.1 = (bf16[4,128,128]{2,1,0:T(8,128)(2,1)S(1)}, bf16[4,128,128]{2,1,0:T(8,128)(2,1)S(1)}, u32[]{:S(2)}, u32[]{:S(2)}) collective-permute-start(bf16[4,128,128]{2,1,0:T(8,128)(2,1)S(1)} %convert_element_type.10), channel_id=1, source_target_pairs={{0,1},{1,0},{2,3},{3,2},{4,5},{5,4},{6,7},{7,6},{8,9},{9,8},{10,11... | collective-permute-start | bytes 393224 | tf_op jit(solution)/shard_map/ppermute | solution.py:24
  98.0 66.4 %collective-permute-start.3 = (f32[136,128]{1,0:T(8,128)S(1)}, f32[136,128]{1,0:T(8,128)S(1)}, u32[]{:S(2)}, u32[]{:S(2)}) collective-permute-start(f32[136,128]{1,0:T(8,128)S(1)} %pad_maximum_fusion), channel_id=1, source_target_pairs={{0,2},{2,0},{4,6},{6,4},{8,10},{10,8},{12,14},{14,12},{1,3},{3,1},... | collective-permute-start | bytes 208904 | tf_op jit(solution)/shard_map/ppermute | solution.py:24
  122.2 7.0 %copy-start.2 = (bf16[1,1,640,128,128]{4,3,2,1,0:T(8,128)(2,1)S(1)}, bf16[1,1,640,128,128]{4,3,2,1,0:T(8,128)(2,1)}, u32[]{:S(2)}) copy-start(bf16[1,1,640,128,128]{4,3,2,1,0:T(8,128)(2,1)} %param.11) | copy-start | bytes 62914564
  129.2 1.2 copy-start.3
  137.1 52.7 %all-to-all-start.2 = ((bf16[8,2,128,128]{3,2,1,0:T(8,128)(2,1)}), bf16[8,2,128,128]{3,2,1,0:T(8,128)(2,1)S(1)}, u32[]{:S(2)}, u32[]{:S(2)}) async-start(bf16[8,2,128,128]{3,2,1,0:T(8,128)(2,1)} %bitcast.6), calls=%async_computation.2 | async-start | bytes 1048576 | tf_op jit(solution)/shard_map/all_to_all | solution.py:28
  164.4 4.4 %collective-permute-start.4 = (f32[136,128]{1,0:T(8,128)S(1)}, f32[136,128]{1,0:T(8,128)S(1)}, u32[]{:S(2)}, u32[]{:S(2)}) collective-permute-start(f32[136,128]{1,0:T(8,128)S(1)} %fusion), channel_id=1, source_target_pairs={{0,4},{2,6},{4,0},{6,2},{8,12},{10,14},{12,8},{14,10},{1,5},{3,7},... | collective-permute-start | bytes 208904 | tf_op jit(solution)/shard_map/ppermute | solution.py:24
  168.8 5.9 %collective-permute-start.5 = (f32[136,128]{1,0:T(8,128)S(1)}, f32[136,128]{1,0:T(8,128)S(1)}, u32[]{:S(2)}, u32[]{:S(2)}) collective-permute-start(f32[136,128]{1,0:T(8,128)S(1)} %add.27), channel_id=1, source_target_pairs={{0,8},{2,10},{4,12},{6,14},{8,0},{10,2},{12,4},{14,6},{1,9},{3,11}... | collective-permute-start | bytes 208904 | tf_op jit(solution)/shard_map/ppermute | solution.py:24
  174.7 4.8 %collective-permute-start.6 = (f32[136,128]{1,0:T(8,128)S(1)}, f32[136,128]{1,0:T(8,128)S(1)}, u32[]{:S(2)}, u32[]{:S(2)}) collective-permute-start(f32[136,128]{1,0:T(8,128)S(1)} %add.28), channel_id=1, source_target_pairs={{0,16},{16,0},{32,48},{48,32},{64,80},{80,64},{96,112},{112,96},{1... | collective-permute-start | bytes 208904 | tf_op jit(solution)/shard_map/ppermute | solution.py:24
  179.5 4.4 %collective-permute-start.7 = (f32[136,128]{1,0:T(8,128)S(1)}, f32[136,128]{1,0:T(8,128)S(1)}, u32[]{:S(2)}, u32[]{:S(2)}) collective-permute-start(f32[136,128]{1,0:T(8,128)S(1)} %add.29), channel_id=1, source_target_pairs={{0,32},{16,48},{32,0},{48,16},{64,96},{80,112},{96,64},{112,80},{1... | collective-permute-start | bytes 208904 | tf_op jit(solution)/shard_map/ppermute | solution.py:24
  183.9 5.9 %collective-permute-start.8 = (f32[136,128]{1,0:T(8,128)S(1)}, f32[136,128]{1,0:T(8,128)S(1)}, u32[]{:S(2)}, u32[]{:S(2)}) collective-permute-start(f32[136,128]{1,0:T(8,128)S(1)} %add.30), channel_id=1, source_target_pairs={{0,64},{16,80},{32,96},{48,112},{64,0},{80,16},{96,32},{112,48},{1... | collective-permute-start | bytes 208904 | tf_op jit(solution)/shard_map/ppermute | solution.py:24
  190.0 5.8 %collective-permute-start.2 = (bf16[2,128,128]{2,1,0:T(8,128)(2,1)S(1)}, bf16[2,128,128]{2,1,0:T(8,128)(2,1)S(1)}, u32[]{:S(2)}, u32[]{:S(2)}) collective-permute-start(bf16[2,128,128]{2,1,0:T(8,128)(2,1)S(1)} %get-tuple-element.23), channel_id=1, source_target_pairs={{0,1},{1,0},{2,3},{3,2},{4,5},{5,4},{6,7},{7,6},{8,9},{9,8},{10,11... | collective-permute-start | bytes 196616 | tf_op jit(solution)/shard_map/ppermute | solution.py:24
Sparse Core Ops, SparseCore 0:
  98.1 24.1 all-gather.2

commit v2 on v1

v2 whole, which is shorter than its diff:
```python
import functools

import jax
import jax.numpy as jnp
from jax import lax
from jax.experimental import pallas as pl
from jax.experimental.pallas import tpu as pltpu
from jax.sharding import PartitionSpec as P

F32 = jnp.float32
BF16 = jnp.bfloat16
TILE = 128
QUAD = 4
STEP = 8
PER = QUAD * STEP
VMEM = pl.BlockSpec(memory_space=pltpu.VMEM)
SMEM = pl.BlockSpec(memory_space=pltpu.SMEM)
ANY = pl.BlockSpec(memory_space=pl.ANY)
PARAMS = pltpu.CompilerParams(vmem_limit_bytes=8 * 1024 * 1024)
PICK_PARAMS = pltpu.CompilerParams(vmem_limit_bytes=16 * 1024 * 1024)


def swap(values, axis, mask):
    size = lax.axis_size(axis)
    return lax.ppermute(values, axis, [(i, i ^ mask) for i in range(size)])


def near(values):
    return pltpu.with_memory_space_constraint(values, pltpu.VMEM)


def iota(shape, dim):
    return lax.broadcasted_iota(jnp.int32, shape, dim)


def order(key, used, source, item, n_keys, length):
    n = key.shape[1]
    hit = ((iota((n_keys, n), 0) == key) & used).astype(F32)
    upto = (iota((n, n), 0) <= iota((n, n), 1)).astype(BF16)
    rank = jnp.dot(hit.astype(BF16), upto, preferred_element_type=F32)
    quads = jnp.floor((rank[:, n - 1 :] + (QUAD - 1)) * (1.0 / QUAD))
    below = (iota((n_keys, n_keys), 0) >= iota((n_keys, n_keys), 1)).astype(BF16)
    wide = jnp.broadcast_to(quads, (n_keys, TILE)).astype(BF16)
    end = jnp.dot(below, wide, preferred_element_type=F32)[:, :1]
    first = (end - quads) * QUAD
    slot = jnp.sum(hit * (first + rank - 1.0), axis=0, keepdims=True)
    slot = jnp.where(used, slot.astype(jnp.int32), -1)
    at = (iota((length, n), 0) == slot).astype(F32).astype(BF16)
    line = iota((8, n), 0)
    values = jnp.where(line == 2, source, 1)
    values = jnp.where(line == 0, item & 255, jnp.where(line == 1, item >> 8, values))
    found = lax.dot_general(
        values.astype(F32).astype(BF16), at, (((1,), (1,)), ((), ())), preferred_element_type=F32
    ).astype(jnp.int32)
    passed = (end * QUAD).astype(jnp.int32) <= iota((n_keys, length), 1)
    target = jnp.sum(passed.astype(F32), axis=0, keepdims=True).astype(jnp.int32)
    items = jnp.where(found[3:4] > 0, found[0:1] + found[1:2] * 256, -1)
    steps = (jnp.max(end).astype(jnp.int32) + STEP - 1) // STEP
    return items, found[2:3], target, steps, slot


def pick_kernel(n_out, n_back, count, ids, rows, columns, fetched, forward, backward, steps):
    row, column = rows[0], columns[0]
    index = iota(row.shape, 1)
    length = forward.shape[1]
    used = (index < count[0, 0]) & (((column >> 1) & 1) == ids[0])
    place = (column >> 2) * 2 + (column & 1)
    owner = jnp.bitwise_xor(row >> 2, ids[1])
    items, source, target, steps[0], slot = order(row, used, place, index, n_out, length)
    fetched[...] = jnp.maximum(items, 0)
    here = jnp.where(items >= 0, iota(items.shape, 1), length)
    forward[...] = here + source * 1024 + target * 65536
    items, source, target, steps[1], slot = order(
        place, used, owner * 4 + (row & 3), slot, n_back, length
    )
    here = jnp.where(items >= 0, items, length)
    backward[...] = here + source * 1024 + target * 65536


def pick(count, ids, rows, columns, n_out, n_back):
    length = rows.shape[-1] + max(n_out, n_back) * (QUAD - 1) + PER
    length = -(-length // TILE) * TILE
    slots = jax.ShapeDtypeStruct((1, length), jnp.int32)
    return pl.pallas_call(
        functools.partial(pick_kernel, n_out, n_back),
        out_shape=[slots, slots, slots, jax.ShapeDtypeStruct((2,), jnp.int32)],
        in_specs=[SMEM, SMEM, VMEM, VMEM],
        out_specs=[VMEM, VMEM, VMEM, SMEM],
        compiler_params=PICK_PARAMS,
        name="pick_tiles",
    )(count, ids, rows, columns)


def stage_kernel(steps, fetched, tiles, held, arrived):
    held[held.shape[0] - 1] = jnp.zeros((TILE, TILE), BF16)

    def start(g, carry):
        for j in range(PER):
            source = tiles.at[fetched[0, g * PER + j]]
            pltpu.make_async_copy(source, held.at[g * PER + j], arrived.at[g]).start()
        return carry

    def finish(g, carry):
        block = held.at[pl.ds(g * PER, PER)]
        pltpu.make_async_copy(tiles.at[pl.ds(0, PER)], block, arrived.at[g]).wait()
        return carry

    lax.fori_loop(0, steps[0], start, 0)
    lax.fori_loop(0, steps[0], finish, 0)


def stage(steps, fetched, tiles):
    length = fetched.shape[1]
    return pl.pallas_call(
        stage_kernel,
        out_shape=pltpu.VMEM((length + 1, TILE, TILE), BF16),
        in_specs=[SMEM, SMEM, ANY],
        out_specs=VMEM,
        scratch_shapes=[pltpu.SemaphoreType.DMA((length // PER,))],
        compiler_params=PARAMS,
        name="stage_tiles",
    )(steps, fetched, pltpu.with_memory_space_constraint(tiles, pltpu.HBM))


def add_products(flipped, count, picked, held, source, total):
    total[...] = jnp.zeros_like(total)

    def step(g, carry):
        places = []
        products = []
        for q in range(STEP):
            codes = [picked[0, g * PER + q * QUAD + j] for j in range(QUAD)]
            places.append(codes[0] >> 16)
            mine = [held[code & 1023] for code in codes]
            other = [source[(code >> 10) & 63] for code in codes]
            left, right = (other, mine) if flipped else (mine, other)
            products.append(
                jnp.dot(
                    jnp.concatenate(left, 1),
                    jnp.concatenate(right, 0),
                    preferred_element_type=F32,
                )
            )
        for place, product in zip(places, products):
            total[place] += product
        return carry

    lax.fori_loop(0, count, step, 0)


def forward_kernel(steps, ids, picked, held, source, kept, sent, total):
    add_products(False, steps[0], picked, held, source, total)
    for k in range(kept.shape[0]):
        own = jnp.bitwise_xor(ids[1], 2 * k)
        kept[k] = total[pl.ds(own * 4, 4)]
        sent[k] = total[pl.ds(jnp.bitwise_xor(own, 1) * 4, 4)].astype(BF16)


def tiles_forward(steps, ids, picked, held, source, n_out):
    shape = (n_out // 8, 4, TILE, TILE)
    return pl.pallas_call(
        forward_kernel,
        out_shape=[pltpu.VMEM(shape, F32), pltpu.VMEM(shape, BF16)],
        in_specs=[SMEM, SMEM, SMEM, VMEM, VMEM],
        out_specs=[VMEM] * 2,
        scratch_shapes=[pltpu.VMEM((n_out + 1, TILE, TILE), F32)],
        compiler_params=PARAMS,
        name="tiles_forward",
    )(steps, ids, picked, near(held), near(source))


def backward_kernel(n_back, steps, picked, held, *refs):
    sources, (out, gathered, total) = refs[:-3], refs[-3:]
    for m, source in enumerate(sources):
        gathered[4 * m : 4 * m + 4] = source[...]
    add_products(True, steps[1], picked, held, gathered, total)
    out[...] = total[:n_back].astype(BF16)


def tiles_backward(steps, picked, held, sources, n_back):
    return pl.pallas_call(
        functools.partial(backward_kernel, n_back),
        out_shape=pltpu.VMEM((n_back, TILE, TILE), BF16),
        in_specs=[SMEM, SMEM] + [VMEM] * (1 + len(sources)),
        out_specs=VMEM,
        scratch_shapes=[
            pltpu.VMEM((4 * len(sources), TILE, TILE), BF16),
            pltpu.VMEM((n_back + 1, TILE, TILE), F32),
        ],
        compiler_params=PARAMS,
        name="tiles_backward",
    )(steps, picked, near(held), *[near(values) for values in sources])


def pair_kernel(kept, got, first, *others):
    first[...] = kept[0] + got[0].astype(F32)
    for k, other in enumerate(others):
        other[...] = (kept[k + 1] + got[k + 1].astype(F32)).astype(BF16)


def pair_sum(kept, got):
    shape = kept.shape[1:]
    n = kept.shape[0] - 1
    return pl.pallas_call(
        pair_kernel,
        out_shape=[pltpu.VMEM(shape, F32)] + [pltpu.VMEM(shape, BF16)] * n,
        in_specs=[VMEM] * 2,
        out_specs=[VMEM] * (n + 1),
        compiler_params=PARAMS,
        name="pair_sum",
    )(near(kept), near(got))


def own_kernel(first, a, b, c, total, sent):
    value = first[...] + a[...].astype(F32) + b[...].astype(F32) + c[...].astype(F32)
    total[...] = value
    sent[...] = value.astype(BF16)


def own_sum(first, others):
    return pl.pallas_call(
        own_kernel,
        out_shape=[pltpu.VMEM(first.shape, F32), pltpu.VMEM(first.shape, BF16)],
        in_specs=[VMEM] * 4,
        out_specs=[VMEM] * 2,
        compiler_params=PARAMS,
        name="own_sum",
    )(near(first), *[near(values) for values in others])


def middle_kernel(own, other, weight, bias, cotangent, activations, back, back_sent, grads):
    blocks = own.shape[0]
    rows = blocks * TILE
    sums = (own[...] + other[...].astype(F32)).astype(BF16).reshape(rows, TILE)
    preact = jnp.dot(sums, weight[...], preferred_element_type=F32) + bias[...]
    sigma = jax.nn.sigmoid(preact)
    activations[...] = (preact * sigma).astype(BF16)
    grad = cotangent[...].astype(F32) * (sigma * (1.0 + preact * (1.0 - sigma)))
    grad_pre = grad.astype(BF16)
    grads[0:TILE] = lax.dot_general(
        sums, grad_pre, (((0,), (0,)), ((), ())), preferred_element_type=F32
    )
    total = jnp.sum(grad_pre.astype(F32), axis=0, keepdims=True)
    grads[TILE : TILE + 8] = jnp.broadcast_to(total, (8, TILE))
    for b in range(blocks):
        value = lax.dot_general(
            weight[...],
            grad_pre[b * TILE : (b + 1) * TILE],
            (((1,), (1,)), ((), ())),
            preferred_element_type=F32,
        )
        back[b] = value
        back_sent[b] = value.astype(BF16)


def middle(own, other, weight, bias, cotangent):
    return pl.pallas_call(
        middle_kernel,
        out_shape=[
            jax.ShapeDtypeStruct(cotangent.shape, BF16),
            pltpu.VMEM(own.shape, F32),
            pltpu.VMEM(own.shape, BF16),
            pltpu.VMEM((TILE + 8, TILE), F32),
        ],
        in_specs=[VMEM] * 5,
        out_specs=[VMEM] * 4,
        compiler_params=PARAMS,
        name="middle",
    )(near(own), near(other), weight, bias, cotangent)


def last_kernel(parts, total, sent):
    for b in range(parts.shape[1]):
        value = jnp.sum(parts[:, b].astype(F32), axis=0).T
        total[b * TILE : (b + 1) * TILE] = value
        sent[b * TILE : (b + 1) * TILE] = value.astype(BF16)


def last_sum(parts):
    shape = (parts.shape[1] * TILE, TILE)
    return pl.pallas_call(
        last_kernel,
        out_shape=[pltpu.VMEM(shape, F32), pltpu.VMEM(shape, BF16)],
        in_specs=[VMEM],
        out_specs=[VMEM] * 2,
        compiler_params=PARAMS,
        name="last_sum",
    )(near(parts))


def finish_kernel(ids, own, other, grads, more, features, weight, bias):
    rows = own.shape[0]
    features[pl.ds(ids[0] * rows, rows)] = own[...]
    features[pl.ds((1 - ids[0]) * rows, rows)] = other[...].astype(F32)
    weight[...] = grads[0:TILE] + more[0:TILE]
    bias[...] = grads[TILE : TILE + 1] + more[TILE : TILE + 1]


def finish(ids, own, other, grads, more):
    return pl.pallas_call(
        finish_kernel,
        out_shape=[
            jax.ShapeDtypeStruct((2 * own.shape[0], TILE), F32),
            jax.ShapeDtypeStruct((TILE, TILE), F32),
            jax.ShapeDtypeStruct((1, TILE), F32),
        ],
        in_specs=[SMEM] + [VMEM] * 4,
        out_specs=[VMEM] * 3,
        compiler_params=PARAMS,
        name="finish",
    )(ids, near(own), near(other), near(grads), near(more))


def local(
    features, weight, hidden_bias, adjacency_tiles, tile_rows, tile_columns, tile_count, cotangent
):
    tiles = adjacency_tiles[0, 0]
    n_row, n_col = lax.axis_size("row"), lax.axis_size("col")
    own_rows, fin = features.shape
    blocks = own_rows // TILE
    n_out, n_back = blocks * n_col, blocks // 2 * n_row
    half = lax.axis_index("feat")
    ids = jnp.stack([half, lax.axis_index("col")]).astype(jnp.int32)

    mine = lax.dynamic_slice_in_dim(features, half * (own_rows // 2), own_rows // 2, 0)
    panel = lax.all_to_all(jnp.broadcast_to(mine[None], (n_row,) + mine.shape), "row", 0, 0)
    fetched, forward, backward, steps = pick(tile_count, ids, tile_rows, tile_columns, n_out, n_back)
    held = stage(steps, fetched, tiles)
    held, panel = lax.optimization_barrier((held, panel))

    kept, sent = tiles_forward(steps, ids, forward, held, panel.reshape(n_back, TILE, fin), n_out)
    first, *others = pair_sum(kept, swap(sent, "col", 1))
    others = [swap(other, "col", 2 * k + 2) for k, other in enumerate(others)]
    own, sent = own_sum(first, others)
    other = swap(sent, "feat", 1)
    activations, back, back_sent, grads = middle(own, other, weight, hidden_bias[None], cotangent)

    back_other, more = lax.optimization_barrier((swap(back_sent, "feat", 1), swap(grads, "row", 1)))
    source = (back + back_other.astype(F32)).astype(BF16)
    grads = grads + more
    far = [swap(source, "col", mask) for mask in (2, 6, 4)]
    beside = swap(source, "col", 1)
    *far, more = lax.optimization_barrier((*far, swap(grads, "row", 2)))
    grads = grads + more
    across = [swap(values, "col", 1) for values in far]
    *across, more = lax.optimization_barrier((*across, swap(grads, "row", 4)))
    grads = grads + more
    sources = [source, beside, far[0], across[0], far[2], across[2], far[1], across[1]]
    out = tiles_backward(steps, backward, held, sources, n_back)
    out, more = lax.optimization_barrier((out, swap(grads, "col", 1)))
    grads = grads + more
    parts = lax.all_to_all(out.reshape(n_row, blocks // 2, fin, TILE), "row", 0, 0)
    parts, more = lax.optimization_barrier((parts, swap(grads, "col", 2)))
    grads = grads + more
    own, sent = last_sum(parts)
    other, more = lax.optimization_barrier((swap(sent, "feat", 1), swap(grads, "col", 4)))
    grad_features, grad_weight, grad_bias = finish(ids, own, other, grads, more)
    return (activations, grad_features, grad_weight, grad_bias[0])


def solution(mesh):
    placed = (
        P(("col", "row"), None),
        P(None, "feat"),
        P("feat"),
        P("row", "col", None, None, None),
        P("row", "col", None),
        P("row", "col", None),
        P("row", "col"),
        P(("row", "col"), "feat"),
    )
    return jax.shard_map(
        local,
        mesh=mesh,
        in_specs=placed,
        out_specs=(P(("row", "col"), "feat"), P(("col", "row"), None), P(None, "feat"), P("feat")),
        check_vma=False,
    )
```

time: 203 us -> 116 us (0.57)
  blocking collectives: 45.1 us -> 0 us
  waiting for transfers between devices: 54.4 us -> 34.4 us
  between operations: 14.8 us -> 1.49 us
  starting transfers between devices: 48.9 us -> 36.9 us
  Pallas kernels: 16.7 us -> 22.7 us
  other arithmetic: 4.7 us -> 0.16 us
    all_to_all x1 -> x0, blocking collectives: 45.1 us -> none  [exchange(): return lax.all_to_all(parts, axis, 0, 0)]
    all_gather x1 -> x0, waiting for transfers between devices: 24.2 us -> none  [local(): back_range = lax.all_gather(back_source, 'col', axis=0, tiled=False)]
    all_to_all x2, starting transfers between devices: 33.2 us -> 9.4 us  [the longest x1 5.91 us: local(): lax.all_to_all(jnp.broadcast_to(mine[None], (n_row,) + mine.shape), 'row'...]
    ppermute x9 -> x20, starting transfers between devices: 15.7 us -> 27.5 us  [swap(): return lax.ppermute(values, axis, [(i, i ^ mask) for i in range(size)])]
    pallas_call x5 -> x8, Pallas kernels: 13.8 us -> 20.2 us  [the longest x1 6.02 us: stage(): pl.pallas_call(stage_kernel, out_shape=pltpu.VMEM((length + 1, TILE, TILE...]
    unnamed x2 -> x0, other arithmetic: 2.58 us -> none
    all_to_all x2, waiting for transfers between devices: 2.7 us -> 4.85 us  [the longest x1 4.84 us: local(): lax.all_to_all(out.reshape(n_row, blocks // 2, fin, TILE), 'row', 0, 0)]
    unnamed x18, local copies, waits for them, and re-layouts: 16.7 us -> 18.8 us
  transfers between devices with their start and end apart: 12 -> 22, of which waited for: 10 -> 11; matrix products, arithmetic and copies ran while one was open for 2% -> 0% of each run, Pallas kernels for 5% -> 13%
where the time goes in v2:
time: 116 us; the launch traced here: 115 us
  starting transfers between devices  36.9 us (32%)
  waiting for transfers between devices  34.4 us (30%)
  Pallas kernels  22.7 us (20%)
  local copies, waits for them, and re-layouts  19.7 us (17%)
  between operations  1.49 us (1%)
    ppermute x20, waiting for transfers between devices, swap(): return lax.ppermute(values, axis, [(i, i ^ mask) for i in range(size)])  29.6 us
    ppermute x20, starting transfers between devices, swap(): return lax.ppermute(values, axis, [(i, i ^ mask) for i in range(size)])  27.5 us
    unnamed x18, local copies, waits for them, and re-layouts  18.8 us
    pallas_call x1, Pallas kernels, stage(): pl.pallas_call(stage_kernel, out_shape=pltpu.VMEM((length + 1, TILE, TILE...  6.02 us
    all_to_all x1, starting transfers between devices, local(): lax.all_to_all(jnp.broadcast_to(mine[None], (n_row,) + mine.shape), 'row'...  5.91 us
    pallas_call x1, Pallas kernels, tiles_backward(): pl.pallas_call(functools.partial(backward_kernel, n_back), out_shape=pltp...  5.89 us
    pallas_call x1, Pallas kernels, tiles_forward(): pl.pallas_call(forward_kernel, out_shape=[pltpu.VMEM(shape, F32), pltpu.V...  5.74 us
    all_to_all x1, waiting for transfers between devices, local(): lax.all_to_all(out.reshape(n_row, blocks // 2, fin, TILE), 'row', 0, 0)  4.84 us
  transfers between devices with their start and end apart: 22, of which 11 were waited for; matrix products, arithmetic and copies ran while one was open for 0% of the time, Pallas kernels for 13%

profile of v2, /device:TPU:0, one launch (start us, length us, event | category | flops | bytes accessed | tf_op | source)
XLA Modules:
  0.0 115.4 jit_solution(7510759347172664814)
XLA Ops:
  0.6 0.0 copy-start
  0.7 0.9 copy-done
  1.5 0.9 broadcast_in_dim.4
  2.4 5.9 %all-to-all-start = ((bf16[8,256,128]{2,1,0:T(8,128)(2,1)}), bf16[8,256,128]{2,1,0:T(8,128)(2,1)S(1)}, u32[]{:S(2)}, u32[]{:S(2)}) async-start(bf16[8,256,128]{2,1,0:T(8,128)(2,1)} %broadcast_in_dim.4), calls=%async_computation | async-start | bytes 1048576 | tf_op jit(solution)/shard_map/all_to_all | solution.py:326
  9.0 0.1 pad_add_fusion.ids
  9.1 0.7 copy-done.6
  9.8 0.7 copy-done.7
  10.4 2.5 %pick_tiles.1 = (s32[1,768]{1,0:T(1,128)S(1)}, s32[1,768]{1,0:T(1,128)S(1)}, s32[1,768]{1,0:T(1,128)S(1)}, s32[2]{0:T(128)S(1)}) custom-call(s32[1,1]{1,0:T(1,128)S(6)} %copy.12.count, s32[2]{0:T(128)S(1)} %pad_add_fusion.ids, s32[1,1,640]{2,1,0:T(1,128)S(1)} %copy-done.6, s32[1,1,640]{2,1,0:T(1,128)S(1)} %copy-done.7), custom_call_target="tpu_custom_call" | custom-call | tf_op jit(solution)/shard_map/pick_tiles/pallas_call | solution.py:84
  13.0 0.0 copy-start.4
  13.0 0.0 copy-start.5
  13.0 6.0 %stage_tiles.1.held = bf16[769,128,128]{2,1,0:T(8,128)(2,1)S(1)} custom-call(s32[2]{0:T(128)S(1)} %get-tuple-element.43.steps, s32[1,768]{1,0:T(1,128)S(1)} %get-tuple-element.45.fetched, bf16[640,128,128]{2,1,0:T(8,128)(2,1)} %bitcast.9), custom_call_target="tpu_custom_call" | custom-call | tf_op jit(solution)/shard_map/stage_tiles/pallas_call | solution.py:114
  19.1 8.3 %copy-done.1 = bf16[769,128,128]{2,1,0:T(8,128)(2,1)} copy-done((bf16[769,128,128]{2,1,0:T(8,128)(2,1)}, bf16[769,128,128]{2,1,0:T(8,128)(2,1)S(1)}, u32[]{:S(2)}) %copy-start.1) | copy-done | bytes 25198616
  27.4 0.0 all-to-all-done
  27.4 8.2 %copy-done.2 = bf16[769,128,128]{2,1,0:T(8,128)(2,1)S(1)} copy-done((bf16[769,128,128]{2,1,0:T(8,128)(2,1)S(1)}, bf16[769,128,128]{2,1,0:T(8,128)(2,1)}, u32[]{:S(2)}) %copy-start.2) | copy-done | bytes 25198616
  35.6 5.7 %tiles_forward.1 = (f32[4,4,128,128]{3,2,1,0:T(8,128)S(1)}, bf16[4,4,128,128]{3,2,1,0:T(8,128)(2,1)S(1)}) custom-call(s32[2]{0:T(128)S(1)} %get-tuple-element.43.steps, s32[2]{0:T(128)S(1)} %pad_add_fusion.ids, s32[1,768]{1,0:T(1,128)S(1)} %get-tuple-element.44.picked, bf16[769,128,128]{2,1,0:T(8,128)(2,1)S(1)} %copy-done.2, bf16[16,128,128]{2,1,0:T(8,128)(2,1)S(1)} %bitcast.7), custom_call_target="tpu_custom_call" | custom-call | tf_op jit(solution)/shard_map/tiles_forward/pallas_call | solution.py:161
  41.3 0.1 collective-permute-start
  41.4 1.9 %collective-permute-done.got = bf16[4,4,128,128]{3,2,1,0:T(8,128)(2,1)S(1)} collective-permute-done((bf16[4,4,128,128]{3,2,1,0:T(8,128)(2,1)S(1)}, bf16[4,4,128,128]{3,2,1,0:T(8,128)(2,1)S(1)}, u32[]{:S(2)}, u32[]{:S(2)}) %collective-permute-start) | collective-permute-done | bytes 524320 | tf_op jit(solution)/shard_map/ppermute | solution.py:25
  43.3 0.1 pair_sum.1
  43.4 0.1 collective-permute-start.1
  43.5 4.7 %collective-permute-start.2 = (bf16[4,128,128]{2,1,0:T(8,128)(2,1)S(1)}, bf16[4,128,128]{2,1,0:T(8,128)(2,1)S(1)}, u32[]{:S(2)}, u32[]{:S(2)}) collective-permute-start(bf16[4,128,128]{2,1,0:T(8,128)(2,1)S(1)} %get-tuple-element.52), channel_id=1, source_target_pairs={{0,8},{2,10},{4,12},{6,14},{8,0},{10,2},{12,4},{14,6},{1,9},{3,11}... | collective-permute-start | bytes 393224 | tf_op jit(solution)/shard_map/ppermute | solution.py:25
  48.2 0.0 collective-permute-start.3
  48.2 1.2 %collective-permute-done.1.a = bf16[4,128,128]{2,1,0:T(8,128)(2,1)S(1)} collective-permute-done((bf16[4,128,128]{2,1,0:T(8,128)(2,1)S(1)}, bf16[4,128,128]{2,1,0:T(8,128)(2,1)S(1)}, u32[]{:S(2)}, u32[]{:S(2)}) %collective-permute-start.1) | collective-permute-done | bytes 131104 | tf_op jit(solution)/shard_map/ppermute | solution.py:25
  49.4 5.4 %collective-permute-done.2.b = bf16[4,128,128]{2,1,0:T(8,128)(2,1)S(1)} collective-permute-done((bf16[4,128,128]{2,1,0:T(8,128)(2,1)S(1)}, bf16[4,128,128]{2,1,0:T(8,128)(2,1)S(1)}, u32[]{:S(2)}, u32[]{:S(2)}) %collective-permute-start.2) | collective-permute-done | bytes 131104 | tf_op jit(solution)/shard_map/ppermute | solution.py:25
  54.8 2.4 %collective-permute-done.3.c = bf16[4,128,128]{2,1,0:T(8,128)(2,1)S(1)} collective-permute-done((bf16[4,128,128]{2,1,0:T(8,128)(2,1)S(1)}, bf16[4,128,128]{2,1,0:T(8,128)(2,1)S(1)}, u32[]{:S(2)}, u32[]{:S(2)}) %collective-permute-start.3) | collective-permute-done | bytes 131104 | tf_op jit(solution)/shard_map/ppermute | solution.py:25
  57.2 0.1 own_sum.1
  57.2 4.1 %collective-permute-start.4 = (bf16[4,128,128]{2,1,0:T(8,128)(2,1)S(1)}, bf16[4,128,128]{2,1,0:T(8,128)(2,1)S(1)}, u32[]{:S(2)}, u32[]{:S(2)}) collective-permute-start(bf16[4,128,128]{2,1,0:T(8,128)(2,1)S(1)} %get-tuple-element.55), channel_id=1, source_target_pairs={{0,1},{1,0},{2,3},{3,2},{4,5},{5,4},{6,7},{7,6},{8,9},{9,8},{10,11... | collective-permute-start | bytes 393224 | tf_op jit(solution)/shard_map/ppermute | solution.py:25
  61.3 3.2 %collective-permute-done.4.other = bf16[4,128,128]{2,1,0:T(8,128)(2,1)S(1)} collective-permute-done((bf16[4,128,128]{2,1,0:T(8,128)(2,1)S(1)}, bf16[4,128,128]{2,1,0:T(8,128)(2,1)S(1)}, u32[]{:S(2)}, u32[]{:S(2)}) %collective-permute-start.4) | collective-permute-done | bytes 131104 | tf_op jit(solution)/shard_map/ppermute | solution.py:25
  64.5 0.9 middle.1
  65.4 3.3 %collective-permute-start.5 = (bf16[4,128,128]{2,1,0:T(8,128)(2,1)S(1)}, bf16[4,128,128]{2,1,0:T(8,128)(2,1)S(1)}, u32[]{:S(2)}, u32[]{:S(2)}) collective-permute-start(bf16[4,128,128]{2,1,0:T(8,128)(2,1)S(1)} %get-tuple-element.59), channel_id=1, source_target_pairs={{0,1},{1,0},{2,3},{3,2},{4,5},{5,4},{6,7},{7,6},{8,9},{9,8},{10,11... | collective-permute-start | bytes 393224 | tf_op jit(solution)/shard_map/ppermute | solution.py:25
  68.7 0.0 collective-permute-start.6
  68.7 4.3 %collective-permute-done.6 = f32[136,128]{1,0:T(8,128)S(1)} collective-permute-done((f32[136,128]{1,0:T(8,128)S(1)}, f32[136,128]{1,0:T(8,128)S(1)}, u32[]{:S(2)}, u32[]{:S(2)}) %collective-permute-start.6) | collective-permute-done | bytes 69664 | tf_op jit(solution)/shard_map/ppermute | solution.py:25
  73.0 0.0 collective-permute-done.5
  73.1 0.1 collective-permute-start.10
  73.1 1.6 %collective-permute-start.9 = (bf16[4,128,128]{2,1,0:T(8,128)(2,1)S(1)}, bf16[4,128,128]{2,1,0:T(8,128)(2,1)S(1)}, u32[]{:S(2)}, u32[]{:S(2)}) collective-permute-start(bf16[4,128,128]{2,1,0:T(8,128)(2,1)S(1)} %add_convert_fusion.refs_0_), channel_id=1, source_target_pairs={{0,12},{2,14},{4,8},{6,10},{8,4},{10,6},{12,0},{14,2},{1,13},{3,15... | collective-permute-start | bytes 393224 | tf_op jit(solution)/shard_map/ppermute | solution.py:25
  74.7 1.9 %collective-permute-start.8 = (bf16[4,128,128]{2,1,0:T(8,128)(2,1)S(1)}, bf16[4,128,128]{2,1,0:T(8,128)(2,1)S(1)}, u32[]{:S(2)}, u32[]{:S(2)}) collective-permute-start(bf16[4,128,128]{2,1,0:T(8,128)(2,1)S(1)} %add_convert_fusion.refs_0_), channel_id=1, source_target_pairs={{0,4},{2,6},{4,0},{6,2},{8,12},{10,14},{12,8},{14,10},{1,5},{3,7},... | collective-permute-start | bytes 393224 | tf_op jit(solution)/shard_map/ppermute | solution.py:25
  76.6 1.5 %collective-permute-start.11 = (f32[136,128]{1,0:T(8,128)S(1)}, f32[136,128]{1,0:T(8,128)S(1)}, u32[]{:S(2)}, u32[]{:S(2)}) collective-permute-start(f32[136,128]{1,0:T(8,128)S(1)} %add.23), channel_id=1, source_target_pairs={{0,32},{16,48},{32,0},{48,16},{64,96},{80,112},{96,64},{112,80},{1... | collective-permute-start | bytes 208904 | tf_op jit(solution)/shard_map/ppermute | solution.py:25
  78.1 2.9 %collective-permute-done.11 = f32[136,128]{1,0:T(8,128)S(1)} collective-permute-done((f32[136,128]{1,0:T(8,128)S(1)}, f32[136,128]{1,0:T(8,128)S(1)}, u32[]{:S(2)}, u32[]{:S(2)}) %collective-permute-start.11) | collective-permute-done | bytes 69664 | tf_op jit(solution)/shard_map/ppermute | solution.py:25
  81.0 0.0 collective-permute-done.10.refs_4_
  81.0 0.0 collective-permute-done.9.refs_6_
  81.0 0.0 collective-permute-done.8.refs_2_
  81.0 0.1 collective-permute-start.12
  81.1 0.5 collective-permute-start.13
  81.6 0.1 collective-permute-start.14
  81.7 3.6 %collective-permute-start.15 = (f32[136,128]{1,0:T(8,128)S(1)}, f32[136,128]{1,0:T(8,128)S(1)}, u32[]{:S(2)}, u32[]{:S(2)}) collective-permute-start(f32[136,128]{1,0:T(8,128)S(1)} %add.24), channel_id=1, source_target_pairs={{0,64},{16,80},{32,96},{48,112},{64,0},{80,16},{96,32},{112,48},{1... | collective-permute-start | bytes 208904 | tf_op jit(solution)/shard_map/ppermute | solution.py:25
  85.3 0.2 collective-permute-start.7
  85.5 2.6 %collective-permute-done.15 = f32[136,128]{1,0:T(8,128)S(1)} collective-permute-done((f32[136,128]{1,0:T(8,128)S(1)}, f32[136,128]{1,0:T(8,128)S(1)}, u32[]{:S(2)}, u32[]{:S(2)}) %collective-permute-start.15) | collective-permute-done | bytes 69664 | tf_op jit(solution)/shard_map/ppermute | solution.py:25
  88.1 0.0 collective-permute-done.12.refs_3_
  88.1 0.0 collective-permute-done.13.refs_7_
  88.1 0.0 collective-permute-done.14.refs_5_
  88.1 0.1 collective-permute-start.16
  88.2 0.0 collective-permute-done.7.refs_1_
  88.2 0.0 copy-done.3
  88.2 5.9 %tiles_backward.1 = bf16[16,128,128]{2,1,0:T(8,128)(2,1)} custom-call(s32[2]{0:T(128)S(1)} %get-tuple-element.43.steps, s32[1,768]{1,0:T(1,128)S(1)} %get-tuple-element.57.picked, bf16[769,128,128]{2,1,0:T(8,128)(2,1)S(1)} %copy-done.3, bf16[4,128,128]{2,1,0:T(8,128)(2,1)S(1)} %add_convert_fusion.refs_0_, ...), custom_call_target="tpu_custom_call" | custom-call | tf_op jit(solution)/shard_map/tiles_backward/pallas_call | solution.py:181
  94.1 0.0 collective-permute-done.16
  94.1 3.5 %all-to-all-start.1 = ((bf16[8,2,128,128]{3,2,1,0:T(8,128)(2,1)}), bf16[8,2,128,128]{3,2,1,0:T(8,128)(2,1)S(1)}, u32[]{:S(2)}, u32[]{:S(2)}) async-start(bf16[8,2,128,128]{3,2,1,0:T(8,128)(2,1)} %bitcast.5), calls=%async_computation.1 | async-start | bytes 1048576 | tf_op jit(solution)/shard_map/all_to_all | solution.py:352
  97.6 2.4 %collective-permute-start.17 = (f32[136,128]{1,0:T(8,128)S(1)}, f32[136,128]{1,0:T(8,128)S(1)}, u32[]{:S(2)}, u32[]{:S(2)}) collective-permute-start(f32[136,128]{1,0:T(8,128)S(1)} %add.26), channel_id=1, source_target_pairs={{0,4},{2,6},{4,0},{6,2},{8,12},{10,14},{12,8},{14,10},{1,5},{3,7},... | collective-permute-start | bytes 208904 | tf_op jit(solution)/shard_map/ppermute | solution.py:25
  100.1 2.8 %collective-permute-done.17 = f32[136,128]{1,0:T(8,128)S(1)} collective-permute-done((f32[136,128]{1,0:T(8,128)S(1)}, f32[136,128]{1,0:T(8,128)S(1)}, u32[]{:S(2)}, u32[]{:S(2)}) %collective-permute-start.17) | collective-permute-done | bytes 69664 | tf_op jit(solution)/shard_map/ppermute | solution.py:25
  102.8 4.8 %all-to-all-done.1.parts = bf16[8,2,128,128]{3,2,1,0:T(8,128)(2,1)S(1)} async-done(((bf16[8,2,128,128]{3,2,1,0:T(8,128)(2,1)}), bf16[8,2,128,128]{3,2,1,0:T(8,128)(2,1)S(1)}, u32[]{:S(2)}, u32[]{:S(2)}) %all-to-all-start.1) | async-done | bytes 524320 | tf_op jit(solution)/shard_map/all_to_all | solution.py:352
  107.7 0.1 collective-permute-start.19
  107.8 0.1 last_sum.1
  107.9 3.2 %collective-permute-start.18 = (bf16[256,128]{1,0:T(8,128)(2,1)S(1)}, bf16[256,128]{1,0:T(8,128)(2,1)S(1)}, u32[]{:S(2)}, u32[]{:S(2)}) collective-permute-start(bf16[256,128]{1,0:T(8,128)(2,1)S(1)} %get-tuple-element.75), channel_id=1, source_target_pairs={{0,1},{1,0},{2,3},{3,2},{4,5},{5,4},{6,7},{7,6},{8,9},{9,8},{10,11... | collective-permute-start | bytes 196616 | tf_op jit(solution)/shard_map/ppermute | solution.py:25
  111.1 2.9 %collective-permute-done.18.other = bf16[256,128]{1,0:T(8,128)(2,1)S(1)} collective-permute-done((bf16[256,128]{1,0:T(8,128)(2,1)S(1)}, bf16[256,128]{1,0:T(8,128)(2,1)S(1)}, u32[]{:S(2)}, u32[]{:S(2)}) %collective-permute-start.18) | collective-permute-done | bytes 65568 | tf_op jit(solution)/shard_map/ppermute | solution.py:25
  114.1 0.0 collective-permute-done.19.more
  114.1 1.3 %finish.1 = (f32[512,128]{1,0:T(8,128)}, f32[128,128]{1,0:T(8,128)}, f32[1,128]{1,0:T(1,128)}) custom-call(s32[2]{0:T(128)S(1)} %pad_add_fusion.ids, f32[256,128]{1,0:T(8,128)S(1)} %get-tuple-element.74.own, bf16[256,128]{1,0:T(8,128)(2,1)S(1)} %collective-permute-done.18.other, f32[136,128]{1,0:T(8,128)S(1)} %add.27.grads, ...), custom_call_target="tpu_custom_call" | custom-call | tf_op jit(solution)/shard_map/finish/pallas_call | solution.py:300
  (16 shorter events, 0.1 us)
Async XLA Ops:
  0.6 0.9 copy-start
  2.4 24.9 %all-to-all-start = ((bf16[8,256,128]{2,1,0:T(8,128)(2,1)}), bf16[8,256,128]{2,1,0:T(8,128)(2,1)S(1)}, u32[]{:S(2)}, u32[]{:S(2)}) async-start(bf16[8,256,128]{2,1,0:T(8,128)(2,1)} %broadcast_in_dim.4), calls=%async_computation | async-start | bytes 1048576 | tf_op jit(solution)/shard_map/all_to_all | solution.py:326
  9.1 0.7 copy-start.6
  9.8 0.7 copy-start.7
  13.0 51.5 %copy-start.4 = (bf16[512,128]{1,0:T(8,128)(2,1)S(1)}, bf16[512,128]{1,0:T(8,128)(2,1)}, u32[]{:S(2)}) copy-start(bf16[512,128]{1,0:T(8,128)(2,1)} %cotangent.1) | copy-start | bytes 393220
  13.0 51.5 %copy-start.5 = (bf16[128,128]{1,0:T(8,128)(2,1)S(1)}, bf16[128,128]{1,0:T(8,128)(2,1)}, u32[]{:S(2)}) copy-start(bf16[128,128]{1,0:T(8,128)(2,1)} %weight.1) | copy-start | bytes 98308
  19.1 8.3 %copy-start.1 = (bf16[769,128,128]{2,1,0:T(8,128)(2,1)}, bf16[769,128,128]{2,1,0:T(8,128)(2,1)S(1)}, u32[]{:S(2)}) copy-start(bf16[769,128,128]{2,1,0:T(8,128)(2,1)S(1)} %stage_tiles.1.held) | copy-start | bytes 75595776
  27.4 37.1 %copy-start.8 = (f32[128]{0:T(128)S(1)}, f32[128]{0:T(128)}, u32[]{:S(2)}) copy-start(f32[128]{0:T(128)} %param.10) | copy-start | bytes 1540
  27.4 8.2 %copy-start.2 = (bf16[769,128,128]{2,1,0:T(8,128)(2,1)S(1)}, bf16[769,128,128]{2,1,0:T(8,128)(2,1)}, u32[]{:S(2)}) copy-start(bf16[769,128,128]{2,1,0:T(8,128)(2,1)} %copy-done.1) | copy-start | bytes 75595776
  35.6 52.6 %copy-start.3 = (bf16[769,128,128]{2,1,0:T(8,128)(2,1)S(1)}, bf16[769,128,128]{2,1,0:T(8,128)(2,1)}, u32[]{:S(2)}) copy-start(bf16[769,128,128]{2,1,0:T(8,128)(2,1)} %copy-done.1) | copy-start | bytes 75595776
  41.3 2.0 %collective-permute-start = (bf16[4,4,128,128]{3,2,1,0:T(8,128)(2,1)S(1)}, bf16[4,4,128,128]{3,2,1,0:T(8,128)(2,1)S(1)}, u32[]{:S(2)}, u32[]{:S(2)}) collective-permute-start(bf16[4,4,128,128]{3,2,1,0:T(8,128)(2,1)S(1)} %get-tuple-element.49), channel_id=1, source_target_pairs={{0,2},{2,0},{4,6},{6,4},{8,10},{10,8},{12,14},{14,12},{1,3},{3,1},... | collective-permute-start | bytes 1572872 | tf_op jit(solution)/shard_map/ppermute | solution.py:25
  43.4 6.0 %collective-permute-start.1 = (bf16[4,128,128]{2,1,0:T(8,128)(2,1)S(1)}, bf16[4,128,128]{2,1,0:T(8,128)(2,1)S(1)}, u32[]{:S(2)}, u32[]{:S(2)}) collective-permute-start(bf16[4,128,128]{2,1,0:T(8,128)(2,1)S(1)} %get-tuple-element.51), channel_id=1, source_target_pairs={{0,4},{2,6},{4,0},{6,2},{8,12},{10,14},{12,8},{14,10},{1,5},{3,7},... | collective-permute-start | bytes 393224 | tf_op jit(solution)/shard_map/ppermute | solution.py:25
  43.5 11.3 %collective-permute-start.2 = (bf16[4,128,128]{2,1,0:T(8,128)(2,1)S(1)}, bf16[4,128,128]{2,1,0:T(8,128)(2,1)S(1)}, u32[]{:S(2)}, u32[]{:S(2)}) collective-permute-start(bf16[4,128,128]{2,1,0:T(8,128)(2,1)S(1)} %get-tuple-element.52), channel_id=1, source_target_pairs={{0,8},{2,10},{4,12},{6,14},{8,0},{10,2},{12,4},{14,6},{1,9},{3,11}... | collective-permute-start | bytes 393224 | tf_op jit(solution)/shard_map/ppermute | solution.py:25
  48.2 9.0 %collective-permute-start.3 = (bf16[4,128,128]{2,1,0:T(8,128)(2,1)S(1)}, bf16[4,128,128]{2,1,0:T(8,128)(2,1)S(1)}, u32[]{:S(2)}, u32[]{:S(2)}) collective-permute-start(bf16[4,128,128]{2,1,0:T(8,128)(2,1)S(1)} %get-tuple-element.53), channel_id=1, source_target_pairs={{0,12},{2,14},{4,8},{6,10},{8,4},{10,6},{12,0},{14,2},{1,13},{3,15... | collective-permute-start | bytes 393224 | tf_op jit(solution)/shard_map/ppermute | solution.py:25
  57.2 7.2 %collective-permute-start.4 = (bf16[4,128,128]{2,1,0:T(8,128)(2,1)S(1)}, bf16[4,128,128]{2,1,0:T(8,128)(2,1)S(1)}, u32[]{:S(2)}, u32[]{:S(2)}) collective-permute-start(bf16[4,128,128]{2,1,0:T(8,128)(2,1)S(1)} %get-tuple-element.55), channel_id=1, source_target_pairs={{0,1},{1,0},{2,3},{3,2},{4,5},{5,4},{6,7},{7,6},{8,9},{9,8},{10,11... | collective-permute-start | bytes 393224 | tf_op jit(solution)/shard_map/ppermute | solution.py:25
  65.4 7.6 %collective-permute-start.5 = (bf16[4,128,128]{2,1,0:T(8,128)(2,1)S(1)}, bf16[4,128,128]{2,1,0:T(8,128)(2,1)S(1)}, u32[]{:S(2)}, u32[]{:S(2)}) collective-permute-start(bf16[4,128,128]{2,1,0:T(8,128)(2,1)S(1)} %get-tuple-element.59), channel_id=1, source_target_pairs={{0,1},{1,0},{2,3},{3,2},{4,5},{5,4},{6,7},{7,6},{8,9},{9,8},{10,11... | collective-permute-start | bytes 393224 | tf_op jit(solution)/shard_map/ppermute | solution.py:25
  68.7 4.3 %collective-permute-start.6 = (f32[136,128]{1,0:T(8,128)S(1)}, f32[136,128]{1,0:T(8,128)S(1)}, u32[]{:S(2)}, u32[]{:S(2)}) collective-permute-start(f32[136,128]{1,0:T(8,128)S(1)} %get-tuple-element.60), channel_id=1, source_target_pairs={{0,16},{16,0},{32,48},{48,32},{64,80},{80,64},{96,112},{112,96},{1... | collective-permute-start | bytes 208904 | tf_op jit(solution)/shard_map/ppermute | solution.py:25
  73.1 8.0 %collective-permute-start.10 = (bf16[4,128,128]{2,1,0:T(8,128)(2,1)S(1)}, bf16[4,128,128]{2,1,0:T(8,128)(2,1)S(1)}, u32[]{:S(2)}, u32[]{:S(2)}) collective-permute-start(bf16[4,128,128]{2,1,0:T(8,128)(2,1)S(1)} %add_convert_fusion.refs_0_), channel_id=1, source_target_pairs={{0,8},{2,10},{4,12},{6,14},{8,0},{10,2},{12,4},{14,6},{1,9},{3,11}... | collective-permute-start | bytes 393224 | tf_op jit(solution)/shard_map/ppermute | solution.py:25
  73.1 7.9 %collective-permute-start.9 = (bf16[4,128,128]{2,1,0:T(8,128)(2,1)S(1)}, bf16[4,128,128]{2,1,0:T(8,128)(2,1)S(1)}, u32[]{:S(2)}, u32[]{:S(2)}) collective-permute-start(bf16[4,128,128]{2,1,0:T(8,128)(2,1)S(1)} %add_convert_fusion.refs_0_), channel_id=1, source_target_pairs={{0,12},{2,14},{4,8},{6,10},{8,4},{10,6},{12,0},{14,2},{1,13},{3,15... | collective-permute-start | bytes 393224 | tf_op jit(solution)/shard_map/ppermute | solution.py:25
  74.7 6.3 %collective-permute-start.8 = (bf16[4,128,128]{2,1,0:T(8,128)(2,1)S(1)}, bf16[4,128,128]{2,1,0:T(8,128)(2,1)S(1)}, u32[]{:S(2)}, u32[]{:S(2)}) collective-permute-start(bf16[4,128,128]{2,1,0:T(8,128)(2,1)S(1)} %add_convert_fusion.refs_0_), channel_id=1, source_target_pairs={{0,4},{2,6},{4,0},{6,2},{8,12},{10,14},{12,8},{14,10},{1,5},{3,7},... | collective-permute-start | bytes 393224 | tf_op jit(solution)/shard_map/ppermute | solution.py:25
  76.6 4.4 %collective-permute-start.11 = (f32[136,128]{1,0:T(8,128)S(1)}, f32[136,128]{1,0:T(8,128)S(1)}, u32[]{:S(2)}, u32[]{:S(2)}) collective-permute-start(f32[136,128]{1,0:T(8,128)S(1)} %add.23), channel_id=1, source_target_pairs={{0,32},{16,48},{32,0},{48,16},{64,96},{80,112},{96,64},{112,80},{1... | collective-permute-start | bytes 208904 | tf_op jit(solution)/shard_map/ppermute | solution.py:25
  81.0 7.0 %collective-permute-start.12 = (bf16[4,128,128]{2,1,0:T(8,128)(2,1)S(1)}, bf16[4,128,128]{2,1,0:T(8,128)(2,1)S(1)}, u32[]{:S(2)}, u32[]{:S(2)}) collective-permute-start(bf16[4,128,128]{2,1,0:T(8,128)(2,1)S(1)} %collective-permute-done.8.refs_2_), channel_id=1, source_target_pairs={{0,2},{2,0},{4,6},{6,4},{8,10},{10,8},{12,14},{14,12},{1,3},{3,1},... | collective-permute-start | bytes 393224 | tf_op jit(solution)/shard_map/ppermute | solution.py:25
  81.1 6.9 %collective-permute-start.13 = (bf16[4,128,128]{2,1,0:T(8,128)(2,1)S(1)}, bf16[4,128,128]{2,1,0:T(8,128)(2,1)S(1)}, u32[]{:S(2)}, u32[]{:S(2)}) collective-permute-start(bf16[4,128,128]{2,1,0:T(8,128)(2,1)S(1)} %collective-permute-done.9.refs_6_), channel_id=1, source_target_pairs={{0,2},{2,0},{4,6},{6,4},{8,10},{10,8},{12,14},{14,12},{1,3},{3,1},... | collective-permute-start | bytes 393224 | tf_op jit(solution)/shard_map/ppermute | solution.py:25
  81.6 6.4 %collective-permute-start.14 = (bf16[4,128,128]{2,1,0:T(8,128)(2,1)S(1)}, bf16[4,128,128]{2,1,0:T(8,128)(2,1)S(1)}, u32[]{:S(2)}, u32[]{:S(2)}) collective-permute-start(bf16[4,128,128]{2,1,0:T(8,128)(2,1)S(1)} %collective-permute-done.10.refs_4_), channel_id=1, source_target_pairs={{0,2},{2,0},{4,6},{6,4},{8,10},{10,8},{12,14},{14,12},{1,3},{3,1},... | collective-permute-start | bytes 393224 | tf_op jit(solution)/shard_map/ppermute | solution.py:25
  81.7 6.3 %collective-permute-start.15 = (f32[136,128]{1,0:T(8,128)S(1)}, f32[136,128]{1,0:T(8,128)S(1)}, u32[]{:S(2)}, u32[]{:S(2)}) collective-permute-start(f32[136,128]{1,0:T(8,128)S(1)} %add.24), channel_id=1, source_target_pairs={{0,64},{16,80},{32,96},{48,112},{64,0},{80,16},{96,32},{112,48},{1... | collective-permute-start | bytes 208904 | tf_op jit(solution)/shard_map/ppermute | solution.py:25
  85.3 2.9 %collective-permute-start.7 = (bf16[4,128,128]{2,1,0:T(8,128)(2,1)S(1)}, bf16[4,128,128]{2,1,0:T(8,128)(2,1)S(1)}, u32[]{:S(2)}, u32[]{:S(2)}) collective-permute-start(bf16[4,128,128]{2,1,0:T(8,128)(2,1)S(1)} %add_convert_fusion.refs_0_), channel_id=1, source_target_pairs={{0,2},{2,0},{4,6},{6,4},{8,10},{10,8},{12,14},{14,12},{1,3},{3,1},... | collective-permute-start | bytes 393224 | tf_op jit(solution)/shard_map/ppermute | solution.py:25
  88.1 6.0 %collective-permute-start.16 = (f32[136,128]{1,0:T(8,128)S(1)}, f32[136,128]{1,0:T(8,128)S(1)}, u32[]{:S(2)}, u32[]{:S(2)}) collective-permute-start(f32[136,128]{1,0:T(8,128)S(1)} %add.25), channel_id=1, source_target_pairs={{0,2},{2,0},{4,6},{6,4},{8,10},{10,8},{12,14},{14,12},{1,3},{3,1},... | collective-permute-start | bytes 208904 | tf_op jit(solution)/shard_map/ppermute | solution.py:25
  94.1 13.6 %all-to-all-start.1 = ((bf16[8,2,128,128]{3,2,1,0:T(8,128)(2,1)}), bf16[8,2,128,128]{3,2,1,0:T(8,128)(2,1)S(1)}, u32[]{:S(2)}, u32[]{:S(2)}) async-start(bf16[8,2,128,128]{3,2,1,0:T(8,128)(2,1)} %bitcast.5), calls=%async_computation.1 | async-start | bytes 1048576 | tf_op jit(solution)/shard_map/all_to_all | solution.py:352
  97.6 5.2 %collective-permute-start.17 = (f32[136,128]{1,0:T(8,128)S(1)}, f32[136,128]{1,0:T(8,128)S(1)}, u32[]{:S(2)}, u32[]{:S(2)}) collective-permute-start(f32[136,128]{1,0:T(8,128)S(1)} %add.26), channel_id=1, source_target_pairs={{0,4},{2,6},{4,0},{6,2},{8,12},{10,14},{12,8},{14,10},{1,5},{3,7},... | collective-permute-start | bytes 208904 | tf_op jit(solution)/shard_map/ppermute | solution.py:25
  107.7 6.4 %collective-permute-start.19 = (f32[136,128]{1,0:T(8,128)S(1)}, f32[136,128]{1,0:T(8,128)S(1)}, u32[]{:S(2)}, u32[]{:S(2)}) collective-permute-start(f32[136,128]{1,0:T(8,128)S(1)} %add.27.grads), channel_id=1, source_target_pairs={{0,8},{2,10},{4,12},{6,14},{8,0},{10,2},{12,4},{14,6},{1,9},{3,11}... | collective-permute-start | bytes 208904 | tf_op jit(solution)/shard_map/ppermute | solution.py:25
  107.9 6.1 %collective-permute-start.18 = (bf16[256,128]{1,0:T(8,128)(2,1)S(1)}, bf16[256,128]{1,0:T(8,128)(2,1)S(1)}, u32[]{:S(2)}, u32[]{:S(2)}) collective-permute-start(bf16[256,128]{1,0:T(8,128)(2,1)S(1)} %get-tuple-element.75), channel_id=1, source_target_pairs={{0,1},{1,0},{2,3},{3,2},{4,5},{5,4},{6,7},{7,6},{8,9},{9,8},{10,11... | collective-permute-start | bytes 196616 | tf_op jit(solution)/shard_map/ppermute | solution.py:25
